TPU v7x, 32 devices: a whole 2x2x4 slice. The times are simulated.
32 devices in a mesh: grp: 2 (over y), seq: 4 (over z), wid: 2 (over x), rep: 2 (over core).
Axes of the slice: x: 2, y: 2, z: 4, core: 2. Of those that a mesh axis runs over, the one named last changes fastest.
Arguments:
- activations: bfloat16 [8192, 8192], P(('grp', 'seq'), ('wid', 'rep')), parts along dimension 0, may hold values from -6 to 6
- output_grads: bfloat16 [8192, 8192], P(('grp', 'seq'), ('wid', 'rep')), parts along dimension 0, may hold values from -6 to 6
- act_exponents: int32 [128, 64], P(('grp', 'seq'), ('wid', 'rep')), parts along dimension 0, may hold values from -2 to 2
- grad_exponents: int32 [128, 64], P(('grp', 'seq'), ('wid', 'rep')), parts along dimension 0, may hold values from -2 to 2
- input_blocks: bfloat16 [16, 128, 64], P(('wid', 'rep')), may hold values from -0.125 to 0.125
- input_index: int32 [16], P(('wid', 'rep')), may hold values from 0 to 63, as said below
- output_blocks: bfloat16 [16, 128, 64], P(('wid', 'rep')), may hold values from -0.125 to 0.125
- output_index: int32 [16], P(('wid', 'rep')), may hold values from 0 to 63, as said below
- fisher_inverse: float32 [4096, 4096], P('seq', 'wid'), may hold values from -1 to 7, as said below
Outputs:
- preconditioned: float32 [64, 2, 4096], P(('grp', 'wid'), 'rep', 'seq'), parts along dimension 0
There are 2 independent parts, one for each index of `grp`. A program takes and returns all parts, laid end to end along the dimension named above; an argument that names none is the same for every part. Nothing has to cross between parts.
Inputs may be any that keep to these rules, and one draw needn't show every extreme that they name: `input_index`: Rising; exactly one index in each aligned run of 4 blocks; the first block and the last block are always named. `output_index`: Rising; exactly one index in each aligned run of 4 blocks; the first block and the last block are always named. `fisher_inverse`: Symmetric.
All inputs are finite; a program needn't handle non-finite values.
Results may differ from a plain program's by a relative error of at most 0.00045.
Values sent between devices are 32-bit elements; how exact they have to be, the bound alone decides.
No kernel may reach another device: no remote copies, remote signals or barrier semaphores. Data moves between devices by JAX's collectives and lax.ppermute only.
A program may use at most 64 MiB of HBM per device.

v0:
```python
import jax
import jax.numpy as jnp
from jax import lax
from jax.sharding import PartitionSpec as P

BLK = 128
LEN = 64


def select_blocks(values, exponents, index, wid_count, rep_count):
    tok_rows = values.shape[0]
    block_count = values.shape[1] // BLK
    seq_local = tok_rows // LEN
    per_device = seq_local // (wid_count * rep_count)
    local_index = index % block_count
    blocks = values.reshape(seq_local, LEN, block_count, BLK)
    picked = jnp.take(blocks, local_index, axis=2)
    scaling = jnp.exp2(jnp.take(exponents, local_index, axis=1).astype(jnp.float32)).astype(
        jnp.bfloat16
    )
    scaled = picked * scaling[:, None, :, None]
    width = index.shape[0] * BLK
    scaled = scaled.reshape(wid_count, per_device, rep_count, LEN, width)
    return jnp.transpose(scaled, (0, 2, 1, 3, 4)).reshape(tok_rows, width)


def tile_product(piece_rows, fisher_tile):
    return lax.dot_general(
        piece_rows,
        fisher_tile,
        (((1,), (1,)), ((), ())),
        precision=lax.Precision.HIGHEST,
        preferred_element_type=jnp.float32,
    )


def shards(
    activations,
    output_grads,
    act_exponents,
    grad_exponents,
    input_blocks,
    input_index,
    output_blocks,
    output_index,
    fisher_inverse,
):
    wid_count = lax.axis_size("wid")
    rep_count = lax.axis_size("rep")
    width_proj = input_blocks.shape[2]
    picked_acts = select_blocks(activations, act_exponents, input_index, wid_count, rep_count)
    picked_grads = select_blocks(output_grads, grad_exponents, output_index, wid_count, rep_count)
    input_flat = input_blocks.reshape(-1, width_proj)
    output_flat = output_blocks.reshape(-1, width_proj)
    act_part = jnp.dot(picked_acts, input_flat, preferred_element_type=jnp.float32)
    grad_part = jnp.dot(picked_grads, output_flat, preferred_element_type=jnp.float32)
    projected = lax.psum_scatter(
        jnp.concatenate([act_part, grad_part], axis=1),
        ("wid", "rep"),
        scatter_dimension=0,
        tiled=True,
    )
    per_device = projected.shape[0] // LEN
    act_proj = projected[:, :width_proj].reshape(per_device, LEN, width_proj)
    grad_proj = projected[:, width_proj:].reshape(per_device, LEN, width_proj)
    outer = jnp.einsum("lti,ltj->lij", grad_proj, act_proj, precision=lax.Precision.HIGHEST) / LEN
    flat = outer.reshape(per_device, width_proj * width_proj)
    routed = lax.all_to_all(flat, "wid", split_axis=1, concat_axis=0, tiled=True)
    partial_value = tile_product(lax.all_gather(routed, "seq", axis=0, tiled=True), fisher_inverse)
    result = lax.psum_scatter(partial_value, "wid", scatter_dimension=0, tiled=True)
    return result.reshape(result.shape[0], 1, result.shape[1])


def solution(mesh):
    placed = (
        P(("grp", "seq"), ("wid", "rep")),
        P(("grp", "seq"), ("wid", "rep")),
        P(("grp", "seq"), ("wid", "rep")),
        P(("grp", "seq"), ("wid", "rep")),
        P(("wid", "rep"), None, None),
        P(("wid", "rep")),
        P(("wid", "rep"), None, None),
        P(("wid", "rep")),
        P("seq", "wid"),
    )
    return jax.shard_map(
        shards,
        mesh=mesh,
        in_specs=placed,
        out_specs=P(("grp", "wid"), "rep", "seq"),
        check_vma=False,
    )
```

profile of v0, /device:TPU:0, one launch (start us, length us, event | category | flops | bytes accessed | tf_op | source)
XLA Modules:
  0.0 108.2 jit_solution(17519123632938801612)
XLA Ops:
  6.5 0.0 copy-start
  6.5 0.0 reduce-scatter.3.cloned.1.call-start
  6.5 3.6 %copy.43 = bf16[128,8,16,128]{3,2,1,0:T(8,128)(2,1)S(1)} copy(bf16[128,8,16,128]{3,1,2,0:T(8,128)(2,1)} %bitcast.56) | data formatting | bytes 8388608
  10.2 0.0 copy-start.4
  10.2 0.0 copy-start.2
  10.2 3.1 %copy.30 = bf16[16,64,16,128]{3,1,2,0:T(8,128)(2,1)} copy(bf16[16,64,16,128]{3,2,1,0:T(8,128)(2,1)S(1)} %bitcast.54) | data formatting | bytes 8388608 | tf_op jit(solution)/shard_map/reshape | solution.py:16
  13.2 0.0 copy-done.4
  13.3 0.0 copy-done.2
  13.3 0.1 copy.31
  13.4 2.9 %gather_fusion.2 = bf16[4,16,64,128]{3,2,1,0:T(8,128)(2,1)S(1)} fusion(bf16[16,64,16,128]{3,1,2,0:T(8,128)(2,1)} %copy.30, s32[1024]{0:T(1024)S(1)} %pad_clamp_fusion), kind=kCustom, calls=%fused_computation.2.clone | custom fusion | bytes 2097168 | tf_op jit(solution)/shard_map/jit(_take)/gather | solution.py:17
  16.3 0.6 gather_fusion.3
  16.9 0.1 fusion.9
  16.9 0.2 bitcast_multiply_fusion
  17.1 0.9 copy.32
  18.0 0.4 reshape.55
  18.5 0.1 copy.33
  18.6 3.6 %copy.42 = bf16[128,8,16,128]{3,2,1,0:T(8,128)(2,1)S(1)} copy(bf16[128,8,16,128]{3,1,2,0:T(8,128)(2,1)} %bitcast.57) | data formatting | bytes 8388608
  22.1 0.0 copy-start.5
  22.2 0.0 copy-start.3
  22.2 3.1 %copy.25 = bf16[16,64,16,128]{3,1,2,0:T(8,128)(2,1)} copy(bf16[16,64,16,128]{3,2,1,0:T(8,128)(2,1)S(1)} %bitcast.55) | data formatting | bytes 8388608 | tf_op jit(solution)/shard_map/reshape | solution.py:16
  25.2 0.0 copy-done.5
  25.3 0.0 copy-done.3
  25.3 0.1 copy.26
  25.3 2.9 %gather_fusion = bf16[4,16,64,128]{3,2,1,0:T(8,128)(2,1)S(1)} fusion(bf16[16,64,16,128]{3,1,2,0:T(8,128)(2,1)} %copy.25, s32[1024]{0:T(1024)S(1)} %pad_clamp_fusion.1), kind=kCustom, calls=%fused_computation.clone | custom fusion | bytes 2097168 | tf_op jit(solution)/shard_map/jit(_take)/gather | solution.py:17
  28.3 0.6 gather_fusion.1
  28.9 0.1 fusion.12
  28.9 0.2 bitcast_multiply_fusion.1
  29.1 0.0 copy-start.1
  29.1 0.9 copy.27
  30.0 0.4 reshape.51
  30.5 0.1 copy.28
  30.6 0.4 fusion.1
  31.0 0.4 fusion.4
  31.4 0.8 pad_maximum_fusion
  32.3 0.0 reduce-scatter.3.cloned.1.call-update
  32.3 0.0 reduce-scatter.5.cloned.1.call-start
  32.4 24.4 %reduce-scatter.3.cloned.1.call-done = f32[256,128]{0,1:T(8,128)} async-done(((f32[1024,128]{0,1:T(8,128)}), f32[256,128]{0,1:T(8,128)}) %reduce-scatter.3.cloned.1.call-update) | async-done | bytes 131088 | tf_op jit(solution)/shard_map/reduce_scatter | solution.py:57
  56.8 0.9 fusion.15
  57.7 0.1 copy.39
  57.8 0.1 reshape.58
  57.9 0.3 convolution_multiply_fusion
  58.2 0.1 all_to_all.14
  58.3 6.5 %all_to_all.19 = f32[4,2,2048]{2,0,1:T(4,128)S(1)} all-to-all(f32[4,2,2048]{2,0,1:T(4,128)S(1)} %copy.37), channel_id=1, replica_groups=mesh['grp'=2,'seq'=4,'wid'=2,'rep'=2] {'wid'}, dimensions={1} | all-to-all | bytes 131072 | tf_op jit(solution)/shard_map/all_to_all | solution.py:68
  64.9 13.9 %all_gather.3 = f32[32,2048]{1,0:T(8,128)S(1)} all-gather(f32[8,2048]{1,0:T(8,128)S(1)} %all_to_all.17), channel_id=1, replica_groups=mesh['grp'=2,'seq'=4,'wid'=2,'rep'=2] {'seq'}, dimensions={0}, use_global_device_ids=true | all-gather | bytes 327680 | tf_op jit(solution)/shard_map/all_gather | solution.py:69
  78.7 10.6 %fusion.16 = f32[32,1024]{1,0:T(8,128)} fusion(f32[32,2048]{1,0:T(8,128)S(1)} %all_gather.3, f32[1024,2048]{1,0:T(8,128)} %param.21), kind=kOutput, calls=%fused_computation.38 | convolution fusion | flops 805306368 | bytes 8781824 | tf_op jit(solution)/shard_map/dot_general | solution.py:28
  89.3 0.0 reduce-scatter.5.cloned.1.call-update
  89.3 10.5 %reduce-scatter.5.cloned.1.call-done = f32[16,1024]{1,0:T(8,128)} async-done(((f32[32,1024]{1,0:T(8,128)}), f32[16,1024]{1,0:T(8,128)}) %reduce-scatter.5.cloned.1.call-update) | async-done | bytes 65552 | tf_op jit(solution)/shard_map/reduce_scatter | solution.py:70
  99.8 1.5 %copy.38 = f32[16,1,1024]{2,1,0:T(1,128)} copy(f32[16,1,1024]{2,0,1:T(8,128)} %bitcast.64) | data formatting | bytes 131072 | tf_op jit(solution)/shard_map/reshape | solution.py:71
  (8 shorter events, 0.1 us)
Async XLA Ops:
  6.5 24.0 %copy-start = (bf16[4,128,64]{1,2,0:T(8,128)(2,1)S(1)}, bf16[4,128,64]{1,2,0:T(8,128)(2,1)}, u32[]{:S(2)}) copy-start(bf16[4,128,64]{1,2,0:T(8,128)(2,1)} %param.19) | copy-start | bytes 196612
  6.5 50.3 %reduce-scatter.3.cloned.1.call-start = ((), (), s32[]{:S(2)}) async-start(), calls=%async_computation.3 | async-start | bytes 655360 | tf_op jit(solution)/shard_map/reduce_scatter | solution.py:57
  10.2 3.1 %copy-start.4 = (s32[4]{0:T(128)S(1)}, s32[4]{0:T(128)}, u32[]{:S(2)}) copy-start(s32[4]{0:T(128)} %param.20) | copy-start | bytes 52
  10.2 3.1 %copy-start.2 = (s32[16,16]{1,0:T(8,128)S(1)}, s32[16,16]{1,0:T(8,128)}, u32[]{:S(2)}) copy-start(s32[16,16]{1,0:T(8,128)} %param.16) | copy-start | bytes 3076
  22.1 3.1 %copy-start.5 = (s32[4]{0:T(128)S(1)}, s32[4]{0:T(128)}, u32[]{:S(2)}) copy-start(s32[4]{0:T(128)} %param.18) | copy-start | bytes 52
  22.2 3.1 %copy-start.3 = (s32[16,16]{1,0:T(8,128)S(1)}, s32[16,16]{1,0:T(8,128)}, u32[]{:S(2)}) copy-start(s32[16,16]{1,0:T(8,128)} %param.15) | copy-start | bytes 3076
  29.1 1.9 %copy-start.1 = (bf16[4,128,64]{1,2,0:T(8,128)(2,1)S(1)}, bf16[4,128,64]{1,2,0:T(8,128)(2,1)}, u32[]{:S(2)}) copy-start(bf16[4,128,64]{1,2,0:T(8,128)(2,1)} %param.17) | copy-start | bytes 196612
  32.3 67.5 %reduce-scatter.5.cloned.1.call-start = ((), (), s32[]{:S(2)}) async-start(), calls=%async_computation.4 | async-start | bytes 196608 | tf_op jit(solution)/shard_map/reduce_scatter | solution.py:70
Sparse Core Ops, SparseCore 0:
  32.4 24.3 reduce-scatter.2
  89.5 10.3 reduce-scatter.4
where the time goes:
time: 109 us; the launch traced here: 108 us
  waiting for transfers between devices  34.9 us (32%)
  local copies, waits for them, and re-layouts  26.1 us (24%)
  blocking collectives  20.4 us (19%)
  between operations  13.6 us (12%)
  matrix products  11.7 us (11%)
  other arithmetic  1.38 us (1%)
    reduce_scatter x1, waiting for transfers between devices, shards(): lax.psum_scatter(jnp.concatenate([act_part, grad_part], axis=1), ('wid',...  24.4 us
    all_gather x1, blocking collectives, shards(): lax.all_gather(routed, 'seq', axis=0, tiled=True)  13.9 us
    dot_general x1, matrix products, tile_product(): lax.dot_general(piece_rows, fisher_tile, (((1,), (1,)), ((), ())), precis...  10.6 us
    reduce_scatter x1, waiting for transfers between devices, shards(): lax.psum_scatter(partial_value, 'wid', scatter_dimension=0, tiled=True)  10.5 us
    unnamed x16, local copies, waits for them, and re-layouts  7.37 us
    all_to_all x1, blocking collectives, shards(): lax.all_to_all(flat, 'wid', split_axis=1, concat_axis=0, tiled=True)  6.5 us
    reshape x2, local copies, waits for them, and re-layouts, select_blocks(): blocks = values.reshape(seq_local, LEN, block_count, BLK)  6.13 us
    gather x2, local copies, waits for them, and re-layouts, select_blocks(): picked = jnp.take(blocks, local_index, axis=2)  5.87 us
  transfers between devices with their start and end apart: 2, of which 2 were waited for; matrix products, arithmetic and copies ran while one was open for 0% of the time, Pallas kernels for 0%

commit v1 on v0

v1 whole, which is shorter than its diff:
```python
import functools

import jax
import jax.numpy as jnp
from jax import lax
from jax.experimental import pallas as pl
from jax.experimental.pallas import tpu as pltpu
from jax.sharding import PartitionSpec as P

BLK = 128
LEN = 64
NT = (((1,), (1,)), ((), ()))
F32 = jnp.float32
BF16 = jnp.bfloat16
VMEM = pl.BlockSpec(memory_space=pltpu.VMEM)
SMEM = pl.BlockSpec(memory_space=pltpu.SMEM)
HBM = pl.BlockSpec(memory_space=pltpu.HBM)
PARAMS = pltpu.CompilerParams(vmem_limit_bytes=16 << 20)


def two_parts(x):
    high = x.astype(BF16)
    return high, (x - high.astype(F32)).astype(BF16)


def product(left, right, dims):
    left_high, left_low = two_parts(left)
    right_high, right_low = two_parts(right)
    dot = functools.partial(lax.dot_general, dimension_numbers=dims, preferred_element_type=F32)
    return dot(left_high, right_high) + (dot(left_high, right_low) + dot(left_low, right_high))


def project_kernel(
    other,
    act_index,
    grad_index,
    act_exponents,
    grad_exponents,
    act_blocks,
    grad_blocks,
    acts,
    grads,
    out,
    picked,
    sems,
):
    rep = lax.axis_index("rep")
    parity = 1 - rep if other else rep
    block_count = act_exponents.shape[1]
    chosen = act_index.shape[0]
    pairs = acts.shape[0]
    sides = ((act_index, act_exponents, act_blocks, acts), (grad_index, grad_exponents, grad_blocks, grads))
    locals_ = []
    copies = []
    for side, (index, _, _, values) in enumerate(sides):
        for block in range(chosen):
            local = lax.rem(index[block], block_count)
            columns = pl.ds(pl.multiple_of(local * BLK, BLK), BLK)
            copy = pltpu.make_async_copy(
                values.at[:, parity, :, columns], picked.at[side, block], sems.at[side, block]
            )
            copy.start()
            locals_.append(local)
            copies.append(copy)
    for side, (_, exponents, blocks, _) in enumerate(sides):
        scaled = []
        for block in range(chosen):
            copies[side * chosen + block].wait()
            rows = []
            for pair in range(pairs):
                exponent = exponents[2 * pair + parity, locals_[side * chosen + block]]
                scale = jnp.exp2(jnp.full((LEN, BLK), exponent, jnp.int32).astype(F32)).astype(BF16)
                rows.append(picked[side, block, pair] * scale)
            scaled.append(jnp.concatenate(rows, axis=0))
        weights = jnp.concatenate([blocks[block] for block in range(chosen)], axis=1)
        width = weights.shape[0]
        out[side * width : (side + 1) * width, :] = lax.dot_general(
            weights, jnp.concatenate(scaled, axis=1), NT, preferred_element_type=F32
        )


def project(other, indices, exponents, blocks, values):
    pairs, _, _, features = values[0].shape
    chosen, width, _ = blocks[0].shape
    tokens = pairs * LEN
    return pl.pallas_call(
        functools.partial(project_kernel, other),
        out_shape=jax.ShapeDtypeStruct((2 * width, tokens), F32),
        in_specs=[SMEM] * 4 + [VMEM] * 2 + [HBM] * 2,
        out_specs=VMEM,
        scratch_shapes=[
            pltpu.VMEM((2, chosen, pairs, LEN, BLK), BF16),
            pltpu.SemaphoreType.DMA((2, chosen)),
        ],
        cost_estimate=pl.CostEstimate(
            flops=4 * tokens * chosen * BLK * width,
            bytes_accessed=4 * tokens * chosen * BLK + 8 * tokens * width,
            transcendentals=0,
        ),
        compiler_params=PARAMS,
        name="project_other" if other else "project_own",
    )(*indices, *exponents, *blocks, *values)


def split_kernel(fisher, high, low, held, sems):
    pieces = held.shape[0]
    rows = fisher.shape[0] // pieces
    copies = [
        pltpu.make_async_copy(fisher.at[pl.ds(piece * rows, rows)], held.at[piece], sems.at[piece])
        for piece in range(pieces)
    ]
    for copy in copies:
        copy.start()
    for piece in range(pieces):
        copies[piece].wait()

        @pl.loop(0, rows // 16)
        def _(step):
            part_high, part_low = two_parts(held[piece, pl.ds(step * 16, 16), :])
            target = pl.ds(piece * rows + step * 16, 16)
            high[target, :] = part_high
            low[target, :] = part_low


def split_fisher(fisher):
    rows, columns = fisher.shape
    pieces = 8
    half = jax.ShapeDtypeStruct((rows, columns), BF16)
    return pl.pallas_call(
        split_kernel,
        out_shape=(half, half),
        in_specs=[pl.BlockSpec(memory_space=pl.ANY)],
        out_specs=(VMEM, VMEM),
        scratch_shapes=[
            pltpu.VMEM((pieces, rows // pieces, columns), F32),
            pltpu.SemaphoreType.DMA((pieces,)),
        ],
        cost_estimate=pl.CostEstimate(
            flops=2 * rows * columns, bytes_accessed=8 * rows * columns, transcendentals=0
        ),
        compiler_params=PARAMS,
        name="split_fisher",
    )(fisher)


def message_kernel(width, own, other, *messages):
    wid = lax.axis_index("wid")
    count = len(messages) + 1
    share = width // count
    acts = own[:width, :] + other[:width, :]
    for shift, message in enumerate(messages, 1):
        target = lax.rem(wid + shift, count)
        rows = pl.ds(pl.multiple_of(width + target * share, share), share)
        message[:width, :] = acts
        message[width:, :] = own[rows, :] + other[rows, :]


def make_messages(own, other, wid_count):
    width = own.shape[0] // 2
    shape = jax.ShapeDtypeStruct((width + width // wid_count, own.shape[1]), F32)
    return pl.pallas_call(
        functools.partial(message_kernel, width),
        out_shape=[shape] * (wid_count - 1),
        in_specs=[VMEM] * 2,
        out_specs=[VMEM] * (wid_count - 1),
        compiler_params=PARAMS,
        name="make_messages",
    )(own, other)


def outer_kernel(width, own, other, *rest):
    *messages, out, staged = rest
    wid = lax.axis_index("wid")
    share = width // (len(messages) + 1)
    rows = pl.ds(pl.multiple_of(width + wid * share, share), share)
    acts = own[:width, :] + other[:width, :]
    grads = own[rows, :] + other[rows, :]
    for message in messages:
        acts = acts + message[:width, :]
        grads = grads + message[width:, :]
    half = share // 2
    pairs = acts.shape[1] // BLK
    lane = lax.broadcasted_iota(jnp.int32, (half, BLK), 1)
    for pair in range(pairs):
        columns = slice(pair * BLK, (pair + 1) * BLK)
        staged[pair] = grads[:, columns]
        pieces = []
        for odd in range(2):
            part = staged[pair, pl.ds(odd, half, stride=2), :]
            pieces.append(jnp.where(lane < LEN, part, 0.0))
            pieces.append(jnp.where(lane < LEN, 0.0, part))
        left = jnp.concatenate(pieces, axis=0)
        result = product(left, acts[:, columns], NT) * (1.0 / LEN)
        both = jnp.concatenate([result[: 2 * half, :], result[2 * half :, :]], axis=1)
        out[pl.ds(2 * pair, half, stride=2 * pairs), :] = both[:half, :]
        out[pl.ds(2 * pair + 1, half, stride=2 * pairs), :] = both[half:, :]


def outer_products(own, other, messages):
    width = own.shape[0] // 2
    tokens = own.shape[1]
    share = width // (len(messages) + 1)
    sequences = tokens // LEN
    return pl.pallas_call(
        functools.partial(outer_kernel, width),
        out_shape=jax.ShapeDtypeStruct((share // 2 * sequences, 2 * width), F32),
        in_specs=[VMEM] * (2 + len(messages)),
        out_specs=VMEM,
        scratch_shapes=[pltpu.VMEM((tokens // BLK, share, BLK), F32)],
        compiler_params=PARAMS,
        name="outer_products",
    )(own, other, *messages)


def fisher_kernel(wid_count, *refs):
    seq_count = len(refs) - 3 - wid_count
    gathered = refs[:seq_count]
    high, low = refs[seq_count : seq_count + 2]
    outs = refs[seq_count + 2 : seq_count + 2 + wid_count]
    placed = refs[-1]
    seq = lax.axis_index("seq")
    wid = lax.axis_index("wid")
    per_wid = seq_count // wid_count
    sequences = placed.shape[2]
    steps = gathered[0].shape[0] // sequences
    rows = []
    for ref in gathered:
        rows.append(
            jnp.concatenate(
                [ref[step * sequences : (step + 1) * sequences, :] for step in range(steps)], axis=1
            )
        )
    left_high, left_low = two_parts(jnp.concatenate(rows, axis=0))
    both = jnp.concatenate([left_high, left_low], axis=0)
    count = left_high.shape[0]
    main = lax.dot_general(both, high[...], NT, preferred_element_type=F32)
    rest = lax.dot_general(left_high, low[...], NT, preferred_element_type=F32)
    result = main[:count] + (main[count:] + rest)
    for shift in range(seq_count):
        group = lax.rem(seq - shift + seq_count, seq_count)
        target = lax.rem(group // per_wid - wid + wid_count, wid_count)
        placed[target, lax.rem(group, per_wid)] = result[shift * sequences : (shift + 1) * sequences]
    for target, out in enumerate(outs):
        for group in range(per_wid):
            out[group * sequences : (group + 1) * sequences, 0, :] = placed[target, group]


def fisher_product(gathered, high, low, wid_count):
    seq_count = len(gathered)
    rows, columns = high.shape
    sequences = gathered[0].shape[0] * BLK // columns
    per_wid = seq_count // wid_count
    shape = jax.ShapeDtypeStruct((per_wid * sequences, 1, rows), F32)
    return pl.pallas_call(
        functools.partial(fisher_kernel, wid_count),
        out_shape=[shape] * wid_count,
        in_specs=[VMEM] * (seq_count + 2),
        out_specs=[VMEM] * wid_count,
        scratch_shapes=[pltpu.VMEM((wid_count, per_wid, sequences, rows), F32)],
        compiler_params=PARAMS,
        name="fisher_product",
    )(*gathered, high, low)


def shifted(value, axis, shift):
    count = lax.axis_size(axis)
    return lax.ppermute(value, axis, [(i, (i + shift) % count) for i in range(count)])


def shards(
    activations,
    output_grads,
    act_exponents,
    grad_exponents,
    input_blocks,
    input_index,
    output_blocks,
    output_index,
    fisher_inverse,
):
    seq_count = lax.axis_size("seq")
    wid_count = lax.axis_size("wid")
    pairs = activations.shape[0] // LEN // 2
    indices = (input_index, output_index)
    exponents = (act_exponents, grad_exponents)
    blocks = (jnp.swapaxes(input_blocks, 1, 2), jnp.swapaxes(output_blocks, 1, 2))
    values = tuple(v.reshape(pairs, 2, LEN, v.shape[1]) for v in (activations, output_grads))
    sent = project(True, indices, exponents, blocks, values)
    other = shifted(sent, "rep", 1)
    own = project(False, indices, exponents, blocks, values)
    messages = make_messages(own, other, wid_count)
    messages = [shifted(m, "wid", shift) for shift, m in enumerate(messages, 1)]
    high, low = split_fisher(fisher_inverse)
    outer = outer_products(own, other, messages)
    gathered = [outer] + [shifted(outer, "seq", shift) for shift in range(1, seq_count)]
    parts = fisher_product(gathered, high, low, wid_count)
    result = parts[0]
    for shift in range(1, wid_count):
        result = result + shifted(parts[shift], "wid", shift)
    return result


def solution(mesh):
    placed = (
        P(("grp", "seq"), ("wid", "rep")),
        P(("grp", "seq"), ("wid", "rep")),
        P(("grp", "seq"), ("wid", "rep")),
        P(("grp", "seq"), ("wid", "rep")),
        P(("wid", "rep"), None, None),
        P(("wid", "rep")),
        P(("wid", "rep"), None, None),
        P(("wid", "rep")),
        P("seq", "wid"),
    )
    return jax.shard_map(
        shards,
        mesh=mesh,
        in_specs=placed,
        out_specs=P(("grp", "wid"), "rep", "seq"),
        check_vma=False,
    )
```

time: 109 us -> 40 us (0.37)
  waiting for transfers between devices: 34.9 us -> 11.6 us
  blocking collectives: 20.4 us -> 0 us
  local copies, waits for them, and re-layouts: 26.1 us -> 8.77 us
  between operations: 13.6 us -> 0.08 us
  matrix products: 11.7 us -> 0 us
  starting transfers between devices: 0.04 us -> 9.55 us
  Pallas kernels: 0 us -> 8.92 us
    reduce_scatter x2 -> x0, waiting for transfers between devices: 34.9 us -> none  [the longest x1 24.4 us: shards(): lax.psum_scatter(jnp.concatenate([act_part, grad_part], axis=1), ('wid',...]
    all_gather x1 -> x0, blocking collectives: 13.9 us -> none  [shards(): lax.all_gather(routed, 'seq', axis=0, tiled=True)]
    dot_general x4 -> x0, matrix products: 11.7 us -> none  [the longest x1 10.6 us: tile_product(): lax.dot_general(piece_rows, fisher_tile, (((1,), (1,)), ((), ())), precis...]
    ppermute x0 -> x6, waiting for transfers between devices: none -> 11.6 us  [shifted(): lax.ppermute(value, axis, [(i, (i + shift) % count) for i in range(count)])]
    ppermute x0 -> x6, starting transfers between devices: none -> 9.55 us  [shifted(): lax.ppermute(value, axis, [(i, (i + shift) % count) for i in range(count)])]
    pallas_call x0 -> x6, Pallas kernels: none -> 8.92 us  [the longest x2 3.94 us: project(): pl.pallas_call(functools.partial(project_kernel, other), out_shape=jax.Sh...]
    reshape x7 -> x0, local copies, waits for them, and re-layouts: 8.75 us -> none  [the longest x2 6.13 us: select_blocks(): blocks = values.reshape(seq_local, LEN, block_count, BLK)]
    gather x4 -> x0, local copies, waits for them, and re-layouts: 6.99 us -> none  [the longest x2 5.87 us: select_blocks(): picked = jnp.take(blocks, local_index, axis=2)]
  transfers between devices with their start and end apart: 2 -> 6, of which waited for: 2 -> 3; matrix products, arithmetic and copies ran while one was open for 0% -> 0% of each run, Pallas kernels for 0% -> 10%
where the time goes in v1:
time: 40 us; the launch traced here: 39.7 us
  waiting for transfers between devices  11.6 us (29%)
  starting transfers between devices  9.55 us (24%)
  Pallas kernels  8.92 us (22%)
  local copies, waits for them, and re-layouts  8.77 us (22%)
  other arithmetic  0.7 us (2%)
    ppermute x6, waiting for transfers between devices, shifted(): lax.ppermute(value, axis, [(i, (i + shift) % count) for i in range(count)])  11.6 us
    ppermute x6, starting transfers between devices, shifted(): lax.ppermute(value, axis, [(i, (i + shift) % count) for i in range(count)])  9.55 us
    unnamed x20, local copies, waits for them, and re-layouts  8.77 us
    pallas_call x2, Pallas kernels, project(): pl.pallas_call(functools.partial(project_kernel, other), out_shape=jax.Sh...  3.94 us
    pallas_call x1, Pallas kernels, fisher_product(): pl.pallas_call(functools.partial(fisher_kernel, wid_count), out_shape=[sh...  2.61 us
    pallas_call x1, Pallas kernels, split_fisher(): pl.pallas_call(split_kernel, out_shape=(half, half), in_specs=[pl.BlockSp...  2.02 us
  transfers between devices with their start and end apart: 6, of which 3 were waited for; matrix products, arithmetic and copies ran while one was open for 0% of the time, Pallas kernels for 10%

profile of v1, /device:TPU:0, one launch (start us, length us, event | category | flops | bytes accessed | tf_op | source)
XLA Modules:
  0.0 39.7 jit_solution(17883162029917102042)
XLA Ops:
  0.0 0.0 copy-start
  0.0 2.2 %copy-done = bf16[1024,2048]{1,0:T(8,128)(2,1)S(1)} copy-done((bf16[1024,2048]{1,0:T(8,128)(2,1)S(1)}, bf16[1024,2048]{1,0:T(8,128)(2,1)}, u32[]{:S(2)}) %copy-start) | copy-done | bytes 4194328
  2.2 0.0 copy-start.1
  2.2 2.2 %copy-done.1 = bf16[1024,2048]{1,0:T(8,128)(2,1)S(1)} copy-done((bf16[1024,2048]{1,0:T(8,128)(2,1)S(1)}, bf16[1024,2048]{1,0:T(8,128)(2,1)}, u32[]{:S(2)}) %copy-start.1) | copy-done | bytes 4194328
  4.4 0.0 copy-start.2
  4.4 0.8 %copy-done.2 = bf16[4,128,64]{1,2,0:T(8,128)(2,1)S(1)} copy-done((bf16[4,128,64]{1,2,0:T(8,128)(2,1)S(1)}, bf16[4,128,64]{1,2,0:T(8,128)(2,1)}, u32[]{:S(2)}) %copy-start.2) | copy-done | bytes 65560
  5.2 0.0 copy-start.3
  5.2 0.8 %copy-done.3 = bf16[4,128,64]{1,2,0:T(8,128)(2,1)S(1)} copy-done((bf16[4,128,64]{1,2,0:T(8,128)(2,1)S(1)}, bf16[4,128,64]{1,2,0:T(8,128)(2,1)}, u32[]{:S(2)}) %copy-start.3) | copy-done | bytes 65560
  6.1 0.0 copy-start.4
  6.1 0.7 %copy-done.4 = s32[16,16]{1,0:T(8,128)S(1)} copy-done((s32[16,16]{1,0:T(8,128)S(1)}, s32[16,16]{1,0:T(8,128)}, u32[]{:S(2)}) %copy-start.4) | copy-done | bytes 1048
  6.8 0.0 copy-start.5
  6.8 0.7 %copy-done.5 = s32[16,16]{1,0:T(8,128)S(1)} copy-done((s32[16,16]{1,0:T(8,128)S(1)}, s32[16,16]{1,0:T(8,128)}, u32[]{:S(2)}) %copy-start.5) | copy-done | bytes 1048
  7.5 0.0 copy-start.6
  7.5 0.7 %copy-done.6 = s32[4]{0:T(128)S(1)} copy-done((s32[4]{0:T(128)S(1)}, s32[4]{0:T(128)}, u32[]{:S(2)}) %copy-start.6) | copy-done | bytes 40
  8.1 0.0 copy-start.7
  8.1 0.7 %copy-done.7 = s32[4]{0:T(128)S(1)} copy-done((s32[4]{0:T(128)S(1)}, s32[4]{0:T(128)}, u32[]{:S(2)}) %copy-start.7) | copy-done | bytes 40
  8.8 0.0 slice-start
  8.8 2.0 %project_other.1 = f32[128,512]{1,0:T(8,128)S(1)} custom-call(s32[4]{0:T(128)S(1)} %copy-done.6, s32[4]{0:T(128)S(1)} %copy-done.7, s32[16,16]{1,0:T(8,128)S(1)} %copy-done.4, s32[16,16]{1,0:T(8,128)S(1)} %copy-done.5, bf16[4,64,128]{2,1,0:T(8,128)(2,1)S(1)} %bitcast.10, bf16[4,64,128]{2,1,0:T(8,128)(2,1)S(1)} %bitcast.12, ...), custom_call_target="tpu_custom_call" | custom-call | flops 67108864 | bytes 1310720 | tf_op jit(solution)/shard_map/project_other/pallas_call | solution.py:86
  10.7 0.0 slice-start.1
  10.8 0.5 %collective-permute-start = (f32[128,512]{1,0:T(8,128)S(1)}, f32[128,512]{1,0:T(8,128)S(1)}, u32[]{:S(2)}, u32[]{:S(2)}) collective-permute-start(f32[128,512]{1,0:T(8,128)S(1)} %project_other.1), channel_id=1, source_target_pairs={{0,1},{1,0},{2,3},{3,2},{4,5},{5,4},{6,7},{7,6},{8,9},{9,8},{10,11... | collective-permute-start | bytes 786440 | tf_op jit(solution)/shard_map/ppermute | solution.py:267
  11.3 2.0 %project_own.1.own = f32[128,512]{1,0:T(8,128)S(1)} custom-call(s32[4]{0:T(128)S(1)} %copy-done.6, s32[4]{0:T(128)S(1)} %copy-done.7, s32[16,16]{1,0:T(8,128)S(1)} %copy-done.4, s32[16,16]{1,0:T(8,128)S(1)} %copy-done.5, bf16[4,64,128]{2,1,0:T(8,128)(2,1)S(1)} %bitcast.11, bf16[4,64,128]{2,1,0:T(8,128)(2,1)S(1)} %bitcast.13, ...), custom_call_target="tpu_custom_call" | custom-call | flops 67108864 | bytes 1310720 | tf_op jit(solution)/shard_map/project_own/pallas_call | solution.py:86
  13.3 0.0 collective-permute-done.other
  13.3 2.6 %collective-permute-start.1 = (f32[96,512]{1,0:T(8,128)S(1)}, f32[96,512]{1,0:T(8,128)S(1)}, u32[]{:S(2)}, u32[]{:S(2)}) collective-permute-start(f32[96,512]{1,0:T(8,128)S(1)} %make_messages.1), channel_id=1, source_target_pairs={{0,2},{2,0},{1,3},{3,1},{4,6},{6,4},{5,7},{7,5},{8,10},{10,8},{9,1... | collective-permute-start | bytes 589832 | tf_op jit(solution)/shard_map/ppermute | solution.py:267
  15.9 5.6 %collective-permute-done.1.rest_0_ = f32[96,512]{1,0:T(8,128)S(1)} collective-permute-done((f32[96,512]{1,0:T(8,128)S(1)}, f32[96,512]{1,0:T(8,128)S(1)}, u32[]{:S(2)}, u32[]{:S(2)}) %collective-permute-start.1) | collective-permute-done | bytes 196640 | tf_op jit(solution)/shard_map/ppermute | solution.py:267
  21.4 0.3 outer_products.1.refs_0_
  21.8 3.9 %collective-permute-start.4 = (f32[128,128]{1,0:T(8,128)S(1)}, f32[128,128]{1,0:T(8,128)S(1)}, u32[]{:S(2)}, u32[]{:S(2)}) collective-permute-start(f32[128,128]{1,0:T(8,128)S(1)} %outer_products.1.refs_0_), channel_id=1, source_target_pairs={{0,12},{4,0},{8,4},{12,8},{1,13},{5,1},{9,5},{13,9},{2,14},{6,2},{... | collective-permute-start | bytes 196616 | tf_op jit(solution)/shard_map/ppermute | solution.py:267
  25.7 0.0 collective-permute-start.3
  25.7 1.0 %collective-permute-start.2 = (f32[128,128]{1,0:T(8,128)S(1)}, f32[128,128]{1,0:T(8,128)S(1)}, u32[]{:S(2)}, u32[]{:S(2)}) collective-permute-start(f32[128,128]{1,0:T(8,128)S(1)} %outer_products.1.refs_0_), channel_id=1, source_target_pairs={{0,4},{4,8},{8,12},{12,0},{1,5},{5,9},{9,13},{13,1},{2,6},{6,10},{... | collective-permute-start | bytes 196616 | tf_op jit(solution)/shard_map/ppermute | solution.py:267
  26.7 0.0 slice-done
  26.7 0.0 slice-done.1
  26.7 2.0 %split_fisher.1 = (bf16[1024,2048]{1,0:T(8,128)(2,1)S(1)}, bf16[1024,2048]{1,0:T(8,128)(2,1)S(1)}) custom-call(f32[1024,2048]{1,0:T(8,128)S(1)} %bitcast.9), custom_call_target="tpu_custom_call" | custom-call | flops 4194304 | bytes 16777216 | tf_op jit(solution)/shard_map/split_fisher/pallas_call | solution.py:129
  28.7 0.0 collective-permute-done.4.refs_3_
  28.7 3.3 %collective-permute-done.3.refs_2_ = f32[128,128]{1,0:T(8,128)S(1)} collective-permute-done((f32[128,128]{1,0:T(8,128)S(1)}, f32[128,128]{1,0:T(8,128)S(1)}, u32[]{:S(2)}, u32[]{:S(2)}) %collective-permute-start.3) | collective-permute-done | bytes 65568 | tf_op jit(solution)/shard_map/ppermute | solution.py:267
  32.0 0.0 collective-permute-done.2.refs_1_
  32.0 2.6 %fisher_product.1 = (f32[16,1,1024]{2,1,0:T(1,128)S(1)}, f32[16,1,1024]{2,1,0:T(1,128)S(1)}) custom-call(f32[128,128]{1,0:T(8,128)S(1)} %outer_products.1.refs_0_, f32[128,128]{1,0:T(8,128)S(1)} %collective-permute-done.2.refs_1_, f32[128,128]{1,0:T(8,128)S(1)} %collective-permute-done.3.refs_2_, f32[128,128]{1,0:T(8,128)S(1)} %collective-permute-done.4.refs_3_, ...), custom_call_target="tpu_custom_call" | custom-call | tf_op jit(solution)/shard_map/fisher_product/pallas_call | solution.py:254
  34.6 1.6 %collective-permute-start.5 = (f32[16,1,1024]{2,1,0:T(1,128)S(1)}, f32[16,1,1024]{2,1,0:T(1,128)S(1)}, u32[]{:S(2)}, u32[]{:S(2)}) collective-permute-start(f32[16,1,1024]{2,1,0:T(1,128)S(1)} %get-tuple-element.12), channel_id=1, source_target_pairs={{0,2},{2,0},{1,3},{3,1},{4,6},{6,4},{5,7},{7,5},{8,10},{10,8},{9,1... | collective-permute-start | bytes 196616 | tf_op jit(solution)/shard_map/ppermute | solution.py:267
  36.2 2.8 %collective-permute-done.5 = f32[16,1,1024]{2,1,0:T(1,128)S(1)} collective-permute-done((f32[16,1,1024]{2,1,0:T(1,128)S(1)}, f32[16,1,1024]{2,1,0:T(1,128)S(1)}, u32[]{:S(2)}, u32[]{:S(2)}) %collective-permute-start.5) | collective-permute-done | bytes 65568 | tf_op jit(solution)/shard_map/ppermute | solution.py:267
  39.0 0.7 %add.3 = f32[16,1,1024]{2,1,0:T(1,128)} add(f32[16,1,1024]{2,1,0:T(1,128)S(1)} %get-tuple-element.11, f32[16,1,1024]{2,1,0:T(1,128)S(1)} %collective-permute-done.5) | non-fusion elementwise | flops 16384 | bytes 196608 | tf_op jit(solution)/shard_map/add | solution.py:299
  (2 shorter events, 0.0 us)
Async XLA Ops:
  0.0 2.2 %copy-start = (bf16[1024,2048]{1,0:T(8,128)(2,1)S(1)}, bf16[1024,2048]{1,0:T(8,128)(2,1)}, u32[]{:S(2)}) copy-start(bf16[1024,2048]{1,0:T(8,128)(2,1)} %param.9) | copy-start | bytes 12582916
  2.2 2.2 %copy-start.1 = (bf16[1024,2048]{1,0:T(8,128)(2,1)S(1)}, bf16[1024,2048]{1,0:T(8,128)(2,1)}, u32[]{:S(2)}) copy-start(bf16[1024,2048]{1,0:T(8,128)(2,1)} %param.10) | copy-start | bytes 12582916
  4.4 0.8 %copy-start.2 = (bf16[4,128,64]{1,2,0:T(8,128)(2,1)S(1)}, bf16[4,128,64]{1,2,0:T(8,128)(2,1)}, u32[]{:S(2)}) copy-start(bf16[4,128,64]{1,2,0:T(8,128)(2,1)} %param.13) | copy-start | bytes 196612
  5.2 0.8 %copy-start.3 = (bf16[4,128,64]{1,2,0:T(8,128)(2,1)S(1)}, bf16[4,128,64]{1,2,0:T(8,128)(2,1)}, u32[]{:S(2)}) copy-start(bf16[4,128,64]{1,2,0:T(8,128)(2,1)} %param.15) | copy-start | bytes 196612
  6.1 0.7 %copy-start.4 = (s32[16,16]{1,0:T(8,128)S(1)}, s32[16,16]{1,0:T(8,128)}, u32[]{:S(2)}) copy-start(s32[16,16]{1,0:T(8,128)} %act_exponents.3) | copy-start | bytes 3076
  6.8 0.7 %copy-start.5 = (s32[16,16]{1,0:T(8,128)S(1)}, s32[16,16]{1,0:T(8,128)}, u32[]{:S(2)}) copy-start(s32[16,16]{1,0:T(8,128)} %grad_exponents.3) | copy-start | bytes 3076
  7.5 0.7 %copy-start.6 = (s32[4]{0:T(128)S(1)}, s32[4]{0:T(128)}, u32[]{:S(2)}) copy-start(s32[4]{0:T(128)} %act_index.3) | copy-start | bytes 52
  8.1 0.7 %copy-start.7 = (s32[4]{0:T(128)S(1)}, s32[4]{0:T(128)}, u32[]{:S(2)}) copy-start(s32[4]{0:T(128)} %grad_index.3) | copy-start | bytes 52
  8.8 17.9 %slice-start = ((s8[8388608]{0:T(1024)(128)(4,1)}), s8[4194304]{0:T(1024)(128)(4,1)S(1)}, s32[]{:S(2)}) async-start(s8[8388608]{0:T(1024)(128)(4,1)} %bitcast.8), calls=%async_computation | async-start | bytes 8388608
  10.7 15.9 %slice-start.1 = ((s8[8388608]{0:T(1024)(128)(4,1)}), s8[4194304]{0:T(1024)(128)(4,1)S(1)}, s32[]{:S(2)}) async-start(s8[8388608]{0:T(1024)(128)(4,1)} %bitcast.8), calls=%async_computation.1 | async-start | bytes 8388608
  10.8 2.5 %collective-permute-start = (f32[128,512]{1,0:T(8,128)S(1)}, f32[128,512]{1,0:T(8,128)S(1)}, u32[]{:S(2)}, u32[]{:S(2)}) collective-permute-start(f32[128,512]{1,0:T(8,128)S(1)} %project_other.1), channel_id=1, source_target_pairs={{0,1},{1,0},{2,3},{3,2},{4,5},{5,4},{6,7},{7,6},{8,9},{9,8},{10,11... | collective-permute-start | bytes 786440 | tf_op jit(solution)/shard_map/ppermute | solution.py:267
  13.3 8.1 %collective-permute-start.1 = (f32[96,512]{1,0:T(8,128)S(1)}, f32[96,512]{1,0:T(8,128)S(1)}, u32[]{:S(2)}, u32[]{:S(2)}) collective-permute-start(f32[96,512]{1,0:T(8,128)S(1)} %make_messages.1), channel_id=1, source_target_pairs={{0,2},{2,0},{1,3},{3,1},{4,6},{6,4},{5,7},{7,5},{8,10},{10,8},{9,1... | collective-permute-start | bytes 589832 | tf_op jit(solution)/shard_map/ppermute | solution.py:267
  21.8 6.9 %collective-permute-start.4 = (f32[128,128]{1,0:T(8,128)S(1)}, f32[128,128]{1,0:T(8,128)S(1)}, u32[]{:S(2)}, u32[]{:S(2)}) collective-permute-start(f32[128,128]{1,0:T(8,128)S(1)} %outer_products.1.refs_0_), channel_id=1, source_target_pairs={{0,12},{4,0},{8,4},{12,8},{1,13},{5,1},{9,5},{13,9},{2,14},{6,2},{... | collective-permute-start | bytes 196616 | tf_op jit(solution)/shard_map/ppermute | solution.py:267
  25.7 6.3 %collective-permute-start.3 = (f32[128,128]{1,0:T(8,128)S(1)}, f32[128,128]{1,0:T(8,128)S(1)}, u32[]{:S(2)}, u32[]{:S(2)}) collective-permute-start(f32[128,128]{1,0:T(8,128)S(1)} %outer_products.1.refs_0_), channel_id=1, source_target_pairs={{0,8},{4,12},{8,0},{12,4},{1,9},{5,13},{9,1},{13,5},{2,10},{6,14},... | collective-permute-start | bytes 196616 | tf_op jit(solution)/shard_map/ppermute | solution.py:267
  25.7 6.3 %collective-permute-start.2 = (f32[128,128]{1,0:T(8,128)S(1)}, f32[128,128]{1,0:T(8,128)S(1)}, u32[]{:S(2)}, u32[]{:S(2)}) collective-permute-start(f32[128,128]{1,0:T(8,128)S(1)} %outer_products.1.refs_0_), channel_id=1, source_target_pairs={{0,4},{4,8},{8,12},{12,0},{1,5},{5,9},{9,13},{13,1},{2,6},{6,10},{... | collective-permute-start | bytes 196616 | tf_op jit(solution)/shard_map/ppermute | solution.py:267
  34.6 4.3 %collective-permute-start.5 = (f32[16,1,1024]{2,1,0:T(1,128)S(1)}, f32[16,1,1024]{2,1,0:T(1,128)S(1)}, u32[]{:S(2)}, u32[]{:S(2)}) collective-permute-start(f32[16,1,1024]{2,1,0:T(1,128)S(1)} %get-tuple-element.12), channel_id=1, source_target_pairs={{0,2},{2,0},{1,3},{3,1},{4,6},{6,4},{5,7},{7,5},{8,10},{10,8},{9,1... | collective-permute-start | bytes 196616 | tf_op jit(solution)/shard_map/ppermute | solution.py:267

commit v2 on v1

--- a/solution.py
+++ b/solution.py
@@ -13,7 +13,6 @@
 F32 = jnp.float32
 BF16 = jnp.bfloat16
 VMEM = pl.BlockSpec(memory_space=pltpu.VMEM)
-SMEM = pl.BlockSpec(memory_space=pltpu.SMEM)
 HBM = pl.BlockSpec(memory_space=pltpu.HBM)
 PARAMS = pltpu.CompilerParams(vmem_limit_bytes=16 << 20)
 
@@ -30,8 +29,27 @@
     return dot(left_high, right_high) + (dot(left_high, right_low) + dot(left_low, right_high))
 
 
-def project_kernel(
-    other,
+def scaled_rows(rows, scale):
+    return rows * jnp.concatenate([scale] * (rows.shape[0] // scale.shape[0]), axis=0)
+
+
+def project_side(picked, scale_of, weights, side):
+    _, chosen, pairs, _, _ = picked.shape
+    tokens = jnp.concatenate(
+        [
+            jnp.concatenate(
+                [scaled_rows(picked[side, block, pair], scale_of(block, pair)) for pair in range(pairs)],
+                axis=0,
+            )
+            for block in range(chosen)
+        ],
+        axis=1,
+    )
+    factor = jnp.concatenate([weights[side, block] for block in range(chosen)], axis=1)
+    return lax.dot_general(factor, tokens, NT, preferred_element_type=F32)
+
+
+def project_other_kernel(
     act_index,
     grad_index,
     act_exponents,
@@ -40,66 +58,132 @@
     grad_blocks,
     acts,
     grads,
-    out,
-    picked,
+    sent,
+    picked_own,
+    scales_own,
+    weights,
+    index,
+    exponents,
+    picked_other,
+    small_sems,
     sems,
 ):
-    rep = lax.axis_index("rep")
-    parity = 1 - rep if other else rep
-    block_count = act_exponents.shape[1]
-    chosen = act_index.shape[0]
-    pairs = acts.shape[0]
-    sides = ((act_index, act_exponents, act_blocks, acts), (grad_index, grad_exponents, grad_blocks, grads))
-    locals_ = []
-    copies = []
-    for side, (index, _, _, values) in enumerate(sides):
+    own = lax.axis_index("rep")
+    other = 1 - own
+    _, chosen, pairs, _, _ = picked_own.shape
+    block_count = exponents.shape[2]
+    values = (acts, grads)
+    small = []
+    for place, (sources, target) in enumerate(
+        (
+            ((act_index, grad_index), index),
+            ((act_exponents, grad_exponents), exponents),
+            ((act_blocks, grad_blocks), weights),
+        )
+    ):
+        for side, source in enumerate(sources):
+            copy = pltpu.make_async_copy(source, target.at[side], small_sems.at[place, side])
+            copy.start()
+            small.append(copy)
+    local = []
+    for side in range(2):
+        small[side].wait()
+        local.append([lax.rem(index[side, block], block_count) for block in range(chosen)])
+    copies = {}
+    for place, (parity, target) in enumerate(((other, picked_other), (own, picked_own))):
+        for side in range(2):
+            for block in range(chosen):
+                columns = pl.ds(pl.multiple_of(local[side][block] * BLK, BLK), BLK)
+                copy = pltpu.make_async_copy(
+                    values[side].at[:, parity, :, columns],
+                    target.at[side, block],
+                    sems.at[place, side, block],
+                )
+                copy.start()
+                copies[place, side, block] = copy
+    for copy in small[2:]:
+        copy.wait()
+
+    def scale_of(side, block, pair, parity):
+        exponent = exponents[side, 2 * pair + parity, local[side][block]]
+        return jnp.exp2(jnp.full((16, BLK), exponent, jnp.int32).astype(F32)).astype(BF16)
+
+    for side in range(2):
         for block in range(chosen):
-            local = lax.rem(index[block], block_count)
-            columns = pl.ds(pl.multiple_of(local * BLK, BLK), BLK)
-            copy = pltpu.make_async_copy(
-                values.at[:, parity, :, columns], picked.at[side, block], sems.at[side, block]
-            )
-            copy.start()
-            locals_.append(local)
-            copies.append(copy)
-    for side, (_, exponents, blocks, _) in enumerate(sides):
-        scaled = []
+            for pair in range(pairs):
+                scales_own[side, block, pair] = scale_of(side, block, pair, own)
+    width = weights.shape[2]
+    for side in range(2):
         for block in range(chosen):
-            copies[side * chosen + block].wait()
-            rows = []
-            for pair in range(pairs):
-                exponent = exponents[2 * pair + parity, locals_[side * chosen + block]]
-                scale = jnp.exp2(jnp.full((LEN, BLK), exponent, jnp.int32).astype(F32)).astype(BF16)
-                rows.append(picked[side, block, pair] * scale)
-            scaled.append(jnp.concatenate(rows, axis=0))
-        weights = jnp.concatenate([blocks[block] for block in range(chosen)], axis=1)
-        width = weights.shape[0]
-        out[side * width : (side + 1) * width, :] = lax.dot_general(
-            weights, jnp.concatenate(scaled, axis=1), NT, preferred_element_type=F32
+            copies[0, side, block].wait()
+        sent[side * width : (side + 1) * width, :] = project_side(
+            picked_other, lambda block, pair: scale_of(side, block, pair, other), weights, side
         )
-
-
-def project(other, indices, exponents, blocks, values):
+    for side in range(2):
+        for block in range(chosen):
+            copies[1, side, block].wait()
+
+
+def project_other(indices, exponents, blocks, values):
     pairs, _, _, features = values[0].shape
     chosen, width, _ = blocks[0].shape
     tokens = pairs * LEN
-    return pl.pallas_call(
-        functools.partial(project_kernel, other),
+    operands = [
+        pltpu.with_memory_space_constraint(v, pltpu.HBM)
+        for v in (*indices, *exponents, *blocks, *values)
+    ]
+    return pl.pallas_call(
+        project_other_kernel,
+        out_shape=(
+            jax.ShapeDtypeStruct((2 * width, tokens), F32),
+            jax.ShapeDtypeStruct((2, chosen, pairs, LEN, BLK), BF16),
+            jax.ShapeDtypeStruct((2, chosen, pairs, 16, BLK), BF16),
+            jax.ShapeDtypeStruct((2, chosen, width, BLK), BF16),
+        ),
+        in_specs=[HBM] * 8,
+        out_specs=[VMEM] * 4,
+        scratch_shapes=[
+            pltpu.SMEM((2, chosen), jnp.int32),
+            pltpu.SMEM((2, *exponents[0].shape), jnp.int32),
+            pltpu.VMEM((2, chosen, pairs, LEN, BLK), BF16),
+            pltpu.SemaphoreType.DMA((3, 2)),
+            pltpu.SemaphoreType.DMA((2, 2, chosen)),
+        ],
+        cost_estimate=pl.CostEstimate(
+            flops=4 * tokens * chosen * BLK * width,
+            bytes_accessed=8 * tokens * chosen * BLK + 8 * tokens * width,
+            transcendentals=0,
+        ),
+        compiler_params=PARAMS,
+        name="project_other",
+    )(*operands)
+
+
+def project_own_kernel(picked, scales, weights, out):
+    width = weights.shape[2]
+    for side in range(2):
+        out[side * width : (side + 1) * width, :] = project_side(
+            picked, lambda block, pair: scales[side, block, pair], weights, side
+        )
+
+
+def project_own(picked, scales, weights):
+    _, chosen, pairs, _, _ = picked.shape
+    width = weights.shape[2]
+    tokens = pairs * LEN
+    return pl.pallas_call(
+        project_own_kernel,
         out_shape=jax.ShapeDtypeStruct((2 * width, tokens), F32),
-        in_specs=[SMEM] * 4 + [VMEM] * 2 + [HBM] * 2,
+        in_specs=[VMEM] * 3,
         out_specs=VMEM,
-        scratch_shapes=[
-            pltpu.VMEM((2, chosen, pairs, LEN, BLK), BF16),
-            pltpu.SemaphoreType.DMA((2, chosen)),
-        ],
         cost_estimate=pl.CostEstimate(
             flops=4 * tokens * chosen * BLK * width,
             bytes_accessed=4 * tokens * chosen * BLK + 8 * tokens * width,
             transcendentals=0,
         ),
         compiler_params=PARAMS,
-        name="project_other" if other else "project_own",
-    )(*indices, *exponents, *blocks, *values)
+        name="project_own",
+    )(picked, scales, weights)
 
 
 def split_kernel(fisher, high, low, held, sems):
@@ -129,7 +213,7 @@
     return pl.pallas_call(
         split_kernel,
         out_shape=(half, half),
-        in_specs=[pl.BlockSpec(memory_space=pl.ANY)],
+        in_specs=[HBM],
         out_specs=(VMEM, VMEM),
         scratch_shapes=[
             pltpu.VMEM((pieces, rows // pieces, columns), F32),
@@ -140,7 +224,7 @@
         ),
         compiler_params=PARAMS,
         name="split_fisher",
-    )(fisher)
+    )(pltpu.with_memory_space_constraint(fisher, pltpu.HBM))
 
 
 def message_kernel(width, own, other, *messages):
@@ -237,7 +321,7 @@
     rest = lax.dot_general(left_high, low[...], NT, preferred_element_type=F32)
     result = main[:count] + (main[count:] + rest)
     for shift in range(seq_count):
-        group = lax.rem(seq - shift + seq_count, seq_count)
+        group = seq ^ shift
         target = lax.rem(group // per_wid - wid + wid_count, wid_count)
         placed[target, lax.rem(group, per_wid)] = result[shift * sequences : (shift + 1) * sequences]
     for target, out in enumerate(outs):
@@ -265,6 +349,10 @@
 def shifted(value, axis, shift):
     count = lax.axis_size(axis)
     return lax.ppermute(value, axis, [(i, (i + shift) % count) for i in range(count)])
+
+
+def swapped(value, axis, step):
+    return lax.ppermute(value, axis, [(i, i ^ step) for i in range(lax.axis_size(axis))])
 
 
 def shards(
@@ -285,14 +373,16 @@
     exponents = (act_exponents, grad_exponents)
     blocks = (jnp.swapaxes(input_blocks, 1, 2), jnp.swapaxes(output_blocks, 1, 2))
     values = tuple(v.reshape(pairs, 2, LEN, v.shape[1]) for v in (activations, output_grads))
-    sent = project(True, indices, exponents, blocks, values)
+    sent, *held = project_other(indices, exponents, blocks, values)
     other = shifted(sent, "rep", 1)
-    own = project(False, indices, exponents, blocks, values)
+    own = project_own(*held)
     messages = make_messages(own, other, wid_count)
-    messages = [shifted(m, "wid", shift) for shift, m in enumerate(messages, 1)]
+    fisher_inverse, *messages = lax.optimization_barrier((fisher_inverse, *messages))
+    received = [shifted(m, "wid", shift) for shift, m in enumerate(messages, 1)]
     high, low = split_fisher(fisher_inverse)
-    outer = outer_products(own, other, messages)
-    gathered = [outer] + [shifted(outer, "seq", shift) for shift in range(1, seq_count)]
+    own, high, low = lax.optimization_barrier((own, high, low))
+    outer = outer_products(own, other, received)
+    gathered = [outer] + [swapped(outer, "seq", step) for step in range(1, seq_count)]
     parts = fisher_product(gathered, high, low, wid_count)
     result = parts[0]
     for shift in range(1, wid_count):

time: 40 us -> 29.8 us (0.74)
  local copies, waits for them, and re-layouts: 8.77 us -> 0 us
  waiting for transfers between devices: 11.6 us -> 9.7 us
  Pallas kernels: 8.92 us -> 9.68 us
    unnamed x20 -> x0, local copies, waits for them, and re-layouts: 8.77 us -> none
    ppermute x6 -> x3, waiting for transfers between devices: 11.6 us -> 5.04 us  [shifted(): lax.ppermute(value, axis, [(i, (i + shift) % count) for i in range(count)])]
    ppermute x0 -> x3, waiting for transfers between devices: none -> 4.66 us  [swapped(): lax.ppermute(value, axis, [(i, i ^ step) for i in range(lax.axis_size(axi...]
    ppermute x0 -> x3, starting transfers between devices: none -> 4.55 us  [swapped(): lax.ppermute(value, axis, [(i, i ^ step) for i in range(lax.axis_size(axi...]
    ppermute x6 -> x3, starting transfers between devices: 9.55 us -> 5.01 us  [shifted(): lax.ppermute(value, axis, [(i, (i + shift) % count) for i in range(count)])]
    pallas_call x3, Pallas kernels: 5.96 us -> 6.72 us  [the longest x1 3.64 us: split_fisher(): pl.pallas_call(split_kernel, out_shape=(half, half), in_specs=[HBM], out_...]
  transfers between devices with their start and end apart: 6 -> 6, of which waited for: 3 -> 5; matrix products, arithmetic and copies ran while one was open for 0% -> 0% of each run, Pallas kernels for 10% -> 14%
where the time goes in v2:
time: 29.8 us; the launch traced here: 29.7 us
  waiting for transfers between devices  9.7 us (33%)
  Pallas kernels  9.68 us (32%)
  starting transfers between devices  9.55 us (32%)
  other arithmetic  0.7 us (2%)
    ppermute x3, waiting for transfers between devices, shifted(): lax.ppermute(value, axis, [(i, (i + shift) % count) for i in range(count)])  5.04 us
    ppermute x3, starting transfers between devices, shifted(): lax.ppermute(value, axis, [(i, (i + shift) % count) for i in range(count)])  5.01 us
    ppermute x3, waiting for transfers between devices, swapped(): lax.ppermute(value, axis, [(i, i ^ step) for i in range(lax.axis_size(axi...  4.66 us
    ppermute x3, starting transfers between devices, swapped(): lax.ppermute(value, axis, [(i, i ^ step) for i in range(lax.axis_size(axi...  4.55 us
    pallas_call x1, Pallas kernels, split_fisher(): pl.pallas_call(split_kernel, out_shape=(half, half), in_specs=[HBM], out_...  3.64 us
    pallas_call x1, Pallas kernels, project_other(): pl.pallas_call(project_other_kernel, out_shape=(jax.ShapeDtypeStruct((2 *...  2.64 us
    pallas_call x1, Pallas kernels, fisher_product(): pl.pallas_call(functools.partial(fisher_kernel, wid_count), out_shape=[sh...  2.61 us
    add x1, other arithmetic, shards(): result = result + shifted(parts[shift], 'wid', shift)  0.7 us
  transfers between devices with their start and end apart: 6, of which 5 were waited for; matrix products, arithmetic and copies ran while one was open for 0% of the time, Pallas kernels for 14%

profile of v2, /device:TPU:0, one launch (start us, length us, event | category | flops | bytes accessed | tf_op | source)
XLA Modules:
  0.0 29.7 jit_solution(153196897843806704)
XLA Ops:
  0.0 2.6 %project_other.1 = (f32[128,512]{1,0:T(8,128)S(1)}, bf16[2,4,8,64,128]{4,3,2,1,0:T(8,128)(2,1)S(1)}, bf16[2,4,8,16,128]{4,3,2,1,0:T(8,128)(2,1)S(1)}, bf16[2,4,64,128]{3,2,1,0:T(8,128)(2,1)S(1)}) custom-call(s32[4]{0:T(128)} %act_index.1, s32[4]{0:T(128)} %grad_index.1, s32[16,16]{1,0:T(8,128)} %act_exponents.1, s32[16,16]{1,0:T(8,128)} %grad_exponents.1, ...), custom_call_target="tpu_custom_call" | custom-call | flops 67108864 | bytes 2359296 | tf_op jit(solution)/shard_map/project_other/pallas_call | solution.py:135
  2.6 0.5 %collective-permute-start = (f32[128,512]{1,0:T(8,128)S(1)}, f32[128,512]{1,0:T(8,128)S(1)}, u32[]{:S(2)}, u32[]{:S(2)}) collective-permute-start(f32[128,512]{1,0:T(8,128)S(1)} %get-tuple-element.21), channel_id=1, source_target_pairs={{0,1},{1,0},{2,3},{3,2},{4,5},{5,4},{6,7},{7,6},{8,9},{9,8},{10,11... | collective-permute-start | bytes 786440 | tf_op jit(solution)/shard_map/ppermute | solution.py:351
  3.2 0.4 %project_own.1.own = f32[128,512]{1,0:T(8,128)S(1)} custom-call(bf16[2,4,8,64,128]{4,3,2,1,0:T(8,128)(2,1)S(1)} %get-tuple-element.18.picked, bf16[2,4,8,16,128]{4,3,2,1,0:T(8,128)(2,1)S(1)} %get-tuple-element.19.scales, bf16[2,4,64,128]{3,2,1,0:T(8,128)(2,1)S(1)} %get-tuple-element.20.weights), custom_call_target="tpu_custom_call" | custom-call | flops 67108864 | bytes 1310720 | tf_op jit(solution)/shard_map/project_own/pallas_call | solution.py:174
  3.6 0.7 %collective-permute-done.other = f32[128,512]{1,0:T(8,128)S(1)} collective-permute-done((f32[128,512]{1,0:T(8,128)S(1)}, f32[128,512]{1,0:T(8,128)S(1)}, u32[]{:S(2)}, u32[]{:S(2)}) %collective-permute-start) | collective-permute-done | bytes 262176 | tf_op jit(solution)/shard_map/ppermute | solution.py:351
  4.4 2.9 %collective-permute-start.1 = (f32[96,512]{1,0:T(8,128)S(1)}, f32[96,512]{1,0:T(8,128)S(1)}, u32[]{:S(2)}, u32[]{:S(2)}) collective-permute-start(f32[96,512]{1,0:T(8,128)S(1)} %make_messages.1), channel_id=1, source_target_pairs={{0,2},{2,0},{1,3},{3,1},{4,6},{6,4},{5,7},{7,5},{8,10},{10,8},{9,1... | collective-permute-start | bytes 589832 | tf_op jit(solution)/shard_map/ppermute | solution.py:351
  7.3 3.6 %split_fisher.1 = (bf16[1024,2048]{1,0:T(8,128)(2,1)S(1)}, bf16[1024,2048]{1,0:T(8,128)(2,1)S(1)}) custom-call(f32[1024,2048]{1,0:T(8,128)} %fisher), custom_call_target="tpu_custom_call" | custom-call | flops 4194304 | bytes 16777216 | tf_op jit(solution)/shard_map/split_fisher/pallas_call | solution.py:213
  10.9 1.6 %collective-permute-done.1.rest_0_ = f32[96,512]{1,0:T(8,128)S(1)} collective-permute-done((f32[96,512]{1,0:T(8,128)S(1)}, f32[96,512]{1,0:T(8,128)S(1)}, u32[]{:S(2)}, u32[]{:S(2)}) %collective-permute-start.1) | collective-permute-done | bytes 196640 | tf_op jit(solution)/shard_map/ppermute | solution.py:351
  12.5 0.3 %outer_products.1.refs_0_ = f32[128,128]{1,0:T(8,128)S(1)} custom-call(f32[128,512]{1,0:T(8,128)S(1)} %project_own.1.own, f32[128,512]{1,0:T(8,128)S(1)} %collective-permute-done.other, f32[96,512]{1,0:T(8,128)S(1)} %collective-permute-done.1.rest_0_), custom_call_target="tpu_custom_call" | custom-call | tf_op jit(solution)/shard_map/outer_products/pallas_call | solution.py:288
  12.8 3.9 %collective-permute-start.4 = (f32[128,128]{1,0:T(8,128)S(1)}, f32[128,128]{1,0:T(8,128)S(1)}, u32[]{:S(2)}, u32[]{:S(2)}) collective-permute-start(f32[128,128]{1,0:T(8,128)S(1)} %outer_products.1.refs_0_), channel_id=1, source_target_pairs={{0,12},{4,8},{8,4},{12,0},{1,13},{5,9},{9,5},{13,1},{2,14},{6,10},... | collective-permute-start | bytes 196616 | tf_op jit(solution)/shard_map/ppermute | solution.py:355
  16.7 0.0 collective-permute-start.3
  16.7 0.6 %collective-permute-start.2 = (f32[128,128]{1,0:T(8,128)S(1)}, f32[128,128]{1,0:T(8,128)S(1)}, u32[]{:S(2)}, u32[]{:S(2)}) collective-permute-start(f32[128,128]{1,0:T(8,128)S(1)} %outer_products.1.refs_0_), channel_id=1, source_target_pairs={{0,4},{4,0},{8,12},{12,8},{1,5},{5,1},{9,13},{13,9},{2,6},{6,2},{1... | collective-permute-start | bytes 196616 | tf_op jit(solution)/shard_map/ppermute | solution.py:355
  17.4 2.4 %collective-permute-done.4.refs_3_ = f32[128,128]{1,0:T(8,128)S(1)} collective-permute-done((f32[128,128]{1,0:T(8,128)S(1)}, f32[128,128]{1,0:T(8,128)S(1)}, u32[]{:S(2)}, u32[]{:S(2)}) %collective-permute-start.4) | collective-permute-done | bytes 65568 | tf_op jit(solution)/shard_map/ppermute | solution.py:355
  19.7 2.3 %collective-permute-done.3.refs_2_ = f32[128,128]{1,0:T(8,128)S(1)} collective-permute-done((f32[128,128]{1,0:T(8,128)S(1)}, f32[128,128]{1,0:T(8,128)S(1)}, u32[]{:S(2)}, u32[]{:S(2)}) %collective-permute-start.3) | collective-permute-done | bytes 65568 | tf_op jit(solution)/shard_map/ppermute | solution.py:355
  22.0 0.0 collective-permute-done.2.refs_1_
  22.0 2.6 %fisher_product.1 = (f32[16,1,1024]{2,1,0:T(1,128)S(1)}, f32[16,1,1024]{2,1,0:T(1,128)S(1)}) custom-call(f32[128,128]{1,0:T(8,128)S(1)} %outer_products.1.refs_0_, f32[128,128]{1,0:T(8,128)S(1)} %collective-permute-done.2.refs_1_, f32[128,128]{1,0:T(8,128)S(1)} %collective-permute-done.3.refs_2_, f32[128,128]{1,0:T(8,128)S(1)} %collective-permute-done.4.refs_3_, ...), custom_call_target="tpu_custom_call" | custom-call | tf_op jit(solution)/shard_map/fisher_product/pallas_call | solution.py:338
  24.6 1.6 %collective-permute-start.5 = (f32[16,1,1024]{2,1,0:T(1,128)S(1)}, f32[16,1,1024]{2,1,0:T(1,128)S(1)}, u32[]{:S(2)}, u32[]{:S(2)}) collective-permute-start(f32[16,1,1024]{2,1,0:T(1,128)S(1)} %get-tuple-element.30), channel_id=1, source_target_pairs={{0,2},{2,0},{1,3},{3,1},{4,6},{6,4},{5,7},{7,5},{8,10},{10,8},{9,1... | collective-permute-start | bytes 196616 | tf_op jit(solution)/shard_map/ppermute | solution.py:351
  26.2 2.8 %collective-permute-done.5 = f32[16,1,1024]{2,1,0:T(1,128)S(1)} collective-permute-done((f32[16,1,1024]{2,1,0:T(1,128)S(1)}, f32[16,1,1024]{2,1,0:T(1,128)S(1)}, u32[]{:S(2)}, u32[]{:S(2)}) %collective-permute-start.5) | collective-permute-done | bytes 65568 | tf_op jit(solution)/shard_map/ppermute | solution.py:351
  29.0 0.7 %add.3 = f32[16,1,1024]{2,1,0:T(1,128)} add(f32[16,1,1024]{2,1,0:T(1,128)S(1)} %get-tuple-element.29, f32[16,1,1024]{2,1,0:T(1,128)S(1)} %collective-permute-done.5) | non-fusion elementwise | flops 16384 | bytes 196608 | tf_op jit(solution)/shard_map/add | solution.py:389
  (1 shorter events, 0.0 us)
Async XLA Ops:
  2.6 1.7 %collective-permute-start = (f32[128,512]{1,0:T(8,128)S(1)}, f32[128,512]{1,0:T(8,128)S(1)}, u32[]{:S(2)}, u32[]{:S(2)}) collective-permute-start(f32[128,512]{1,0:T(8,128)S(1)} %get-tuple-element.21), channel_id=1, source_target_pairs={{0,1},{1,0},{2,3},{3,2},{4,5},{5,4},{6,7},{7,6},{8,9},{9,8},{10,11... | collective-permute-start | bytes 786440 | tf_op jit(solution)/shard_map/ppermute | solution.py:351
  4.4 8.1 %collective-permute-start.1 = (f32[96,512]{1,0:T(8,128)S(1)}, f32[96,512]{1,0:T(8,128)S(1)}, u32[]{:S(2)}, u32[]{:S(2)}) collective-permute-start(f32[96,512]{1,0:T(8,128)S(1)} %make_messages.1), channel_id=1, source_target_pairs={{0,2},{2,0},{1,3},{3,1},{4,6},{6,4},{5,7},{7,5},{8,10},{10,8},{9,1... | collective-permute-start | bytes 589832 | tf_op jit(solution)/shard_map/ppermute | solution.py:351
  12.8 6.9 %collective-permute-start.4 = (f32[128,128]{1,0:T(8,128)S(1)}, f32[128,128]{1,0:T(8,128)S(1)}, u32[]{:S(2)}, u32[]{:S(2)}) collective-permute-start(f32[128,128]{1,0:T(8,128)S(1)} %outer_products.1.refs_0_), channel_id=1, source_target_pairs={{0,12},{4,8},{8,4},{12,0},{1,13},{5,9},{9,5},{13,1},{2,14},{6,10},... | collective-permute-start | bytes 196616 | tf_op jit(solution)/shard_map/ppermute | solution.py:355
  16.7 5.3 %collective-permute-start.3 = (f32[128,128]{1,0:T(8,128)S(1)}, f32[128,128]{1,0:T(8,128)S(1)}, u32[]{:S(2)}, u32[]{:S(2)}) collective-permute-start(f32[128,128]{1,0:T(8,128)S(1)} %outer_products.1.refs_0_), channel_id=1, source_target_pairs={{0,8},{4,12},{8,0},{12,4},{1,9},{5,13},{9,1},{13,5},{2,10},{6,14},... | collective-permute-start | bytes 196616 | tf_op jit(solution)/shard_map/ppermute | solution.py:355
  16.7 5.3 %collective-permute-start.2 = (f32[128,128]{1,0:T(8,128)S(1)}, f32[128,128]{1,0:T(8,128)S(1)}, u32[]{:S(2)}, u32[]{:S(2)}) collective-permute-start(f32[128,128]{1,0:T(8,128)S(1)} %outer_products.1.refs_0_), channel_id=1, source_target_pairs={{0,4},{4,0},{8,12},{12,8},{1,5},{5,1},{9,13},{13,9},{2,6},{6,2},{1... | collective-permute-start | bytes 196616 | tf_op jit(solution)/shard_map/ppermute | solution.py:355
  24.6 4.3 %collective-permute-start.5 = (f32[16,1,1024]{2,1,0:T(1,128)S(1)}, f32[16,1,1024]{2,1,0:T(1,128)S(1)}, u32[]{:S(2)}, u32[]{:S(2)}) collective-permute-start(f32[16,1,1024]{2,1,0:T(1,128)S(1)} %get-tuple-element.30), channel_id=1, source_target_pairs={{0,2},{2,0},{1,3},{3,1},{4,6},{6,4},{5,7},{7,5},{8,10},{10,8},{9,1... | collective-permute-start | bytes 196616 | tf_op jit(solution)/shard_map/ppermute | solution.py:351

commit v3 on v2

--- a/solution.py
+++ b/solution.py
@@ -9,6 +9,7 @@
 
 BLK = 128
 LEN = 64
+MXU = 256
 NT = (((1,), (1,)), ((), ()))
 F32 = jnp.float32
 BF16 = jnp.bfloat16
@@ -296,6 +297,31 @@
     )(own, other, *messages)
 
 
+def tile_products(left_high, left_low, high, low):
+    rows, columns = high.shape
+    streamed = rows // 4 // MXU * MXU
+    count = left_high.shape[0]
+    both = jnp.concatenate([left_high, left_low], axis=0)
+    dot = functools.partial(lax.dot_general, dimension_numbers=NT, preferred_element_type=F32)
+    sums = None
+    for start in range(0, columns, MXU):
+        piece = slice(start, start + MXU)
+        terms = []
+        if streamed:
+            terms.append(dot(high[:streamed, piece], both[:, piece]))
+        terms.append(dot(both[:, piece], high[streamed:, piece]))
+        if streamed:
+            terms.append(dot(low[:streamed, piece], left_high[:, piece]))
+        terms.append(dot(left_high[:, piece], low[streamed:, piece]))
+        sums = terms if sums is None else [a + b for a, b in zip(sums, terms)]
+    held_high, held_low = sums[1::2] if streamed else sums
+    result = held_high[:count] + (held_high[count:] + held_low)
+    if streamed:
+        tall = sums[0][:, :count] + (sums[0][:, count:] + sums[2])
+        result = jnp.concatenate([tall.T, result], axis=1)
+    return result
+
+
 def fisher_kernel(wid_count, *refs):
     seq_count = len(refs) - 3 - wid_count
     gathered = refs[:seq_count]
@@ -315,11 +341,7 @@
             )
         )
     left_high, left_low = two_parts(jnp.concatenate(rows, axis=0))
-    both = jnp.concatenate([left_high, left_low], axis=0)
-    count = left_high.shape[0]
-    main = lax.dot_general(both, high[...], NT, preferred_element_type=F32)
-    rest = lax.dot_general(left_high, low[...], NT, preferred_element_type=F32)
-    result = main[:count] + (main[count:] + rest)
+    result = tile_products(left_high, left_low, high, low)
     for shift in range(seq_count):
         group = seq ^ shift
         target = lax.rem(group // per_wid - wid + wid_count, wid_count)

time: 29.8 us -> 29.3 us (0.983)
  Pallas kernels: 9.68 us -> 9.18 us
    pallas_call x1, Pallas kernels: 2.61 us -> 2.11 us  [fisher_product(): pl.pallas_call(functools.partial(fisher_kernel, wid_count), out_shape=[sh...]
where the time goes in v3:
time: 29.3 us; the launch traced here: 29.2 us
  waiting for transfers between devices  9.69 us (33%)
  starting transfers between devices  9.56 us (33%)
  Pallas kernels  9.18 us (31%)
  other arithmetic  0.7 us (2%)
    ppermute x3, waiting for transfers between devices, shifted(): lax.ppermute(value, axis, [(i, (i + shift) % count) for i in range(count)])  5.04 us
    ppermute x3, starting transfers between devices, shifted(): lax.ppermute(value, axis, [(i, (i + shift) % count) for i in range(count)])  5.01 us
    ppermute x3, waiting for transfers between devices, swapped(): lax.ppermute(value, axis, [(i, i ^ step) for i in range(lax.axis_size(axi...  4.66 us
    ppermute x3, starting transfers between devices, swapped(): lax.ppermute(value, axis, [(i, i ^ step) for i in range(lax.axis_size(axi...  4.55 us
    pallas_call x1, Pallas kernels, split_fisher(): pl.pallas_call(split_kernel, out_shape=(half, half), in_specs=[HBM], out_...  3.64 us
    pallas_call x1, Pallas kernels, project_other(): pl.pallas_call(project_other_kernel, out_shape=(jax.ShapeDtypeStruct((2 *...  2.64 us
    pallas_call x1, Pallas kernels, fisher_product(): pl.pallas_call(functools.partial(fisher_kernel, wid_count), out_shape=[sh...  2.11 us
    add x1, other arithmetic, shards(): result = result + shifted(parts[shift], 'wid', shift)  0.7 us
  transfers between devices with their start and end apart: 6, of which 5 were waited for; matrix products, arithmetic and copies ran while one was open for 0% of the time, Pallas kernels for 14%

profile of v3, /device:TPU:0, one launch (start us, length us, event | category | flops | bytes accessed | tf_op | source)
XLA Modules:
  0.0 29.2 jit_solution(7788309451534520522)
XLA Ops:
  0.0 2.6 %project_other.1 = (f32[128,512]{1,0:T(8,128)S(1)}, bf16[2,4,8,64,128]{4,3,2,1,0:T(8,128)(2,1)S(1)}, bf16[2,4,8,16,128]{4,3,2,1,0:T(8,128)(2,1)S(1)}, bf16[2,4,64,128]{3,2,1,0:T(8,128)(2,1)S(1)}) custom-call(s32[4]{0:T(128)} %act_index.1, s32[4]{0:T(128)} %grad_index.1, s32[16,16]{1,0:T(8,128)} %act_exponents.1, s32[16,16]{1,0:T(8,128)} %grad_exponents.1, ...), custom_call_target="tpu_custom_call" | custom-call | flops 67108864 | bytes 2359296 | tf_op jit(solution)/shard_map/project_other/pallas_call | solution.py:136
  2.6 0.5 %collective-permute-start = (f32[128,512]{1,0:T(8,128)S(1)}, f32[128,512]{1,0:T(8,128)S(1)}, u32[]{:S(2)}, u32[]{:S(2)}) collective-permute-start(f32[128,512]{1,0:T(8,128)S(1)} %get-tuple-element.21), channel_id=1, source_target_pairs={{0,1},{1,0},{2,3},{3,2},{4,5},{5,4},{6,7},{7,6},{8,9},{9,8},{10,11... | collective-permute-start | bytes 786440 | tf_op jit(solution)/shard_map/ppermute | solution.py:373
  3.2 0.4 %project_own.1.own = f32[128,512]{1,0:T(8,128)S(1)} custom-call(bf16[2,4,8,64,128]{4,3,2,1,0:T(8,128)(2,1)S(1)} %get-tuple-element.18.picked, bf16[2,4,8,16,128]{4,3,2,1,0:T(8,128)(2,1)S(1)} %get-tuple-element.19.scales, bf16[2,4,64,128]{3,2,1,0:T(8,128)(2,1)S(1)} %get-tuple-element.20.weights), custom_call_target="tpu_custom_call" | custom-call | flops 67108864 | bytes 1310720 | tf_op jit(solution)/shard_map/project_own/pallas_call | solution.py:175
  3.6 0.7 %collective-permute-done.other = f32[128,512]{1,0:T(8,128)S(1)} collective-permute-done((f32[128,512]{1,0:T(8,128)S(1)}, f32[128,512]{1,0:T(8,128)S(1)}, u32[]{:S(2)}, u32[]{:S(2)}) %collective-permute-start) | collective-permute-done | bytes 262176 | tf_op jit(solution)/shard_map/ppermute | solution.py:373
  4.4 2.9 %collective-permute-start.1 = (f32[96,512]{1,0:T(8,128)S(1)}, f32[96,512]{1,0:T(8,128)S(1)}, u32[]{:S(2)}, u32[]{:S(2)}) collective-permute-start(f32[96,512]{1,0:T(8,128)S(1)} %make_messages.1), channel_id=1, source_target_pairs={{0,2},{2,0},{1,3},{3,1},{4,6},{6,4},{5,7},{7,5},{8,10},{10,8},{9,1... | collective-permute-start | bytes 589832 | tf_op jit(solution)/shard_map/ppermute | solution.py:373
  7.3 3.6 %split_fisher.1 = (bf16[1024,2048]{1,0:T(8,128)(2,1)S(1)}, bf16[1024,2048]{1,0:T(8,128)(2,1)S(1)}) custom-call(f32[1024,2048]{1,0:T(8,128)} %fisher), custom_call_target="tpu_custom_call" | custom-call | flops 4194304 | bytes 16777216 | tf_op jit(solution)/shard_map/split_fisher/pallas_call | solution.py:214
  10.9 1.6 %collective-permute-done.1.rest_0_ = f32[96,512]{1,0:T(8,128)S(1)} collective-permute-done((f32[96,512]{1,0:T(8,128)S(1)}, f32[96,512]{1,0:T(8,128)S(1)}, u32[]{:S(2)}, u32[]{:S(2)}) %collective-permute-start.1) | collective-permute-done | bytes 196640 | tf_op jit(solution)/shard_map/ppermute | solution.py:373
  12.5 0.3 %outer_products.1.refs_0_ = f32[128,128]{1,0:T(8,128)S(1)} custom-call(f32[128,512]{1,0:T(8,128)S(1)} %project_own.1.own, f32[128,512]{1,0:T(8,128)S(1)} %collective-permute-done.other, f32[96,512]{1,0:T(8,128)S(1)} %collective-permute-done.1.rest_0_), custom_call_target="tpu_custom_call" | custom-call | tf_op jit(solution)/shard_map/outer_products/pallas_call | solution.py:289
  12.8 3.9 %collective-permute-start.4 = (f32[128,128]{1,0:T(8,128)S(1)}, f32[128,128]{1,0:T(8,128)S(1)}, u32[]{:S(2)}, u32[]{:S(2)}) collective-permute-start(f32[128,128]{1,0:T(8,128)S(1)} %outer_products.1.refs_0_), channel_id=1, source_target_pairs={{0,12},{4,8},{8,4},{12,0},{1,13},{5,9},{9,5},{13,1},{2,14},{6,10},... | collective-permute-start | bytes 196616 | tf_op jit(solution)/shard_map/ppermute | solution.py:377
  16.7 0.0 collective-permute-start.3
  16.7 0.6 %collective-permute-start.2 = (f32[128,128]{1,0:T(8,128)S(1)}, f32[128,128]{1,0:T(8,128)S(1)}, u32[]{:S(2)}, u32[]{:S(2)}) collective-permute-start(f32[128,128]{1,0:T(8,128)S(1)} %outer_products.1.refs_0_), channel_id=1, source_target_pairs={{0,4},{4,0},{8,12},{12,8},{1,5},{5,1},{9,13},{13,9},{2,6},{6,2},{1... | collective-permute-start | bytes 196616 | tf_op jit(solution)/shard_map/ppermute | solution.py:377
  17.4 2.4 %collective-permute-done.4.refs_3_ = f32[128,128]{1,0:T(8,128)S(1)} collective-permute-done((f32[128,128]{1,0:T(8,128)S(1)}, f32[128,128]{1,0:T(8,128)S(1)}, u32[]{:S(2)}, u32[]{:S(2)}) %collective-permute-start.4) | collective-permute-done | bytes 65568 | tf_op jit(solution)/shard_map/ppermute | solution.py:377
  19.7 2.3 %collective-permute-done.3.refs_2_ = f32[128,128]{1,0:T(8,128)S(1)} collective-permute-done((f32[128,128]{1,0:T(8,128)S(1)}, f32[128,128]{1,0:T(8,128)S(1)}, u32[]{:S(2)}, u32[]{:S(2)}) %collective-permute-start.3) | collective-permute-done | bytes 65568 | tf_op jit(solution)/shard_map/ppermute | solution.py:377
  22.0 0.0 collective-permute-done.2.refs_1_
  22.0 2.1 %fisher_product.1 = (f32[16,1,1024]{2,1,0:T(1,128)S(1)}, f32[16,1,1024]{2,1,0:T(1,128)S(1)}) custom-call(f32[128,128]{1,0:T(8,128)S(1)} %outer_products.1.refs_0_, f32[128,128]{1,0:T(8,128)S(1)} %collective-permute-done.2.refs_1_, f32[128,128]{1,0:T(8,128)S(1)} %collective-permute-done.3.refs_2_, f32[128,128]{1,0:T(8,128)S(1)} %collective-permute-done.4.refs_3_, ...), custom_call_target="tpu_custom_call" | custom-call | tf_op jit(solution)/shard_map/fisher_product/pallas_call | solution.py:360
  24.1 1.6 %collective-permute-start.5 = (f32[16,1,1024]{2,1,0:T(1,128)S(1)}, f32[16,1,1024]{2,1,0:T(1,128)S(1)}, u32[]{:S(2)}, u32[]{:S(2)}) collective-permute-start(f32[16,1,1024]{2,1,0:T(1,128)S(1)} %get-tuple-element.30), channel_id=1, source_target_pairs={{0,2},{2,0},{1,3},{3,1},{4,6},{6,4},{5,7},{7,5},{8,10},{10,8},{9,1... | collective-permute-start | bytes 196616 | tf_op jit(solution)/shard_map/ppermute | solution.py:373
  25.7 2.8 %collective-permute-done.5 = f32[16,1,1024]{2,1,0:T(1,128)S(1)} collective-permute-done((f32[16,1,1024]{2,1,0:T(1,128)S(1)}, f32[16,1,1024]{2,1,0:T(1,128)S(1)}, u32[]{:S(2)}, u32[]{:S(2)}) %collective-permute-start.5) | collective-permute-done | bytes 65568 | tf_op jit(solution)/shard_map/ppermute | solution.py:373
  28.5 0.7 %add.3 = f32[16,1,1024]{2,1,0:T(1,128)} add(f32[16,1,1024]{2,1,0:T(1,128)S(1)} %get-tuple-element.29, f32[16,1,1024]{2,1,0:T(1,128)S(1)} %collective-permute-done.5) | non-fusion elementwise | flops 16384 | bytes 196608 | tf_op jit(solution)/shard_map/add | solution.py:411
  (1 shorter events, 0.0 us)
Async XLA Ops:
  2.6 1.7 %collective-permute-start = (f32[128,512]{1,0:T(8,128)S(1)}, f32[128,512]{1,0:T(8,128)S(1)}, u32[]{:S(2)}, u32[]{:S(2)}) collective-permute-start(f32[128,512]{1,0:T(8,128)S(1)} %get-tuple-element.21), channel_id=1, source_target_pairs={{0,1},{1,0},{2,3},{3,2},{4,5},{5,4},{6,7},{7,6},{8,9},{9,8},{10,11... | collective-permute-start | bytes 786440 | tf_op jit(solution)/shard_map/ppermute | solution.py:373
  4.4 8.1 %collective-permute-start.1 = (f32[96,512]{1,0:T(8,128)S(1)}, f32[96,512]{1,0:T(8,128)S(1)}, u32[]{:S(2)}, u32[]{:S(2)}) collective-permute-start(f32[96,512]{1,0:T(8,128)S(1)} %make_messages.1), channel_id=1, source_target_pairs={{0,2},{2,0},{1,3},{3,1},{4,6},{6,4},{5,7},{7,5},{8,10},{10,8},{9,1... | collective-permute-start | bytes 589832 | tf_op jit(solution)/shard_map/ppermute | solution.py:373
  12.8 6.9 %collective-permute-start.4 = (f32[128,128]{1,0:T(8,128)S(1)}, f32[128,128]{1,0:T(8,128)S(1)}, u32[]{:S(2)}, u32[]{:S(2)}) collective-permute-start(f32[128,128]{1,0:T(8,128)S(1)} %outer_products.1.refs_0_), channel_id=1, source_target_pairs={{0,12},{4,8},{8,4},{12,0},{1,13},{5,9},{9,5},{13,1},{2,14},{6,10},... | collective-permute-start | bytes 196616 | tf_op jit(solution)/shard_map/ppermute | solution.py:377
  16.7 5.3 %collective-permute-start.3 = (f32[128,128]{1,0:T(8,128)S(1)}, f32[128,128]{1,0:T(8,128)S(1)}, u32[]{:S(2)}, u32[]{:S(2)}) collective-permute-start(f32[128,128]{1,0:T(8,128)S(1)} %outer_products.1.refs_0_), channel_id=1, source_target_pairs={{0,8},{4,12},{8,0},{12,4},{1,9},{5,13},{9,1},{13,5},{2,10},{6,14},... | collective-permute-start | bytes 196616 | tf_op jit(solution)/shard_map/ppermute | solution.py:377
  16.7 5.3 %collective-permute-start.2 = (f32[128,128]{1,0:T(8,128)S(1)}, f32[128,128]{1,0:T(8,128)S(1)}, u32[]{:S(2)}, u32[]{:S(2)}) collective-permute-start(f32[128,128]{1,0:T(8,128)S(1)} %outer_products.1.refs_0_), channel_id=1, source_target_pairs={{0,4},{4,0},{8,12},{12,8},{1,5},{5,1},{9,13},{13,9},{2,6},{6,2},{1... | collective-permute-start | bytes 196616 | tf_op jit(solution)/shard_map/ppermute | solution.py:377
  24.1 4.3 %collective-permute-start.5 = (f32[16,1,1024]{2,1,0:T(1,128)S(1)}, f32[16,1,1024]{2,1,0:T(1,128)S(1)}, u32[]{:S(2)}, u32[]{:S(2)}) collective-permute-start(f32[16,1,1024]{2,1,0:T(1,128)S(1)} %get-tuple-element.30), channel_id=1, source_target_pairs={{0,2},{2,0},{1,3},{3,1},{4,6},{6,4},{5,7},{7,5},{8,10},{10,8},{9,1... | collective-permute-start | bytes 196616 | tf_op jit(solution)/shard_map/ppermute | solution.py:373

commit v4 on v3

--- a/solution.py
+++ b/solution.py
@@ -10,6 +10,7 @@
 BLK = 128
 LEN = 64
 MXU = 256
+PIECES = 8
 NT = (((1,), (1,)), ((), ()))
 F32 = jnp.float32
 BF16 = jnp.bfloat16
@@ -187,9 +188,8 @@
     )(picked, scales, weights)
 
 
-def split_kernel(fisher, high, low, held, sems):
-    pieces = held.shape[0]
-    rows = fisher.shape[0] // pieces
+def split_pieces(fisher, high, low, held, sems):
+    pieces, rows, _ = held.shape
     copies = [
         pltpu.make_async_copy(fisher.at[pl.ds(piece * rows, rows)], held.at[piece], sems.at[piece])
         for piece in range(pieces)
@@ -207,25 +207,39 @@
             low[target, :] = part_low
 
 
-def split_fisher(fisher):
+def split_early_kernel(fisher, high, low, held, sems):
+    @pl.when(lax.axis_index("rep") == 1)
+    def _():
+        split_pieces(fisher, high, low, held, sems)
+
+
+def split_late_kernel(fisher, high_in, low_in, high, low, held, sems):
+    del high_in, low_in
+
+    @pl.when(lax.axis_index("rep") == 0)
+    def _():
+        split_pieces(fisher, high, low, held, sems)
+
+
+def split_fisher(fisher, *halves):
     rows, columns = fisher.shape
-    pieces = 8
     half = jax.ShapeDtypeStruct((rows, columns), BF16)
     return pl.pallas_call(
-        split_kernel,
+        split_late_kernel if halves else split_early_kernel,
         out_shape=(half, half),
-        in_specs=[HBM],
+        in_specs=[HBM] + [VMEM] * len(halves),
         out_specs=(VMEM, VMEM),
         scratch_shapes=[
-            pltpu.VMEM((pieces, rows // pieces, columns), F32),
-            pltpu.SemaphoreType.DMA((pieces,)),
+            pltpu.VMEM((PIECES, rows // PIECES, columns), F32),
+            pltpu.SemaphoreType.DMA((PIECES,)),
         ],
+        input_output_aliases={1: 0, 2: 1} if halves else {},
         cost_estimate=pl.CostEstimate(
             flops=2 * rows * columns, bytes_accessed=8 * rows * columns, transcendentals=0
         ),
         compiler_params=PARAMS,
-        name="split_fisher",
-    )(pltpu.with_memory_space_constraint(fisher, pltpu.HBM))
+        name="split_late" if halves else "split_early",
+    )(pltpu.with_memory_space_constraint(fisher, pltpu.HBM), *halves)
 
 
 def message_kernel(width, own, other, *messages):
@@ -322,6 +336,11 @@
     return result
 
 
+def exchange_steps(seq_count):
+    steps = range(1, seq_count)
+    return list(zip(steps, sorted(steps, key=lambda step: (step.bit_count(), -step))))
+
+
 def fisher_kernel(wid_count, *refs):
     seq_count = len(refs) - 3 - wid_count
     gathered = refs[:seq_count]
@@ -342,8 +361,9 @@
         )
     left_high, left_low = two_parts(jnp.concatenate(rows, axis=0))
     result = tile_products(left_high, left_low, high, low)
-    for shift in range(seq_count):
-        group = seq ^ shift
+    rep = lax.axis_index("rep")
+    for shift, (first, second) in enumerate([(0, 0)] + exchange_steps(seq_count)):
+        group = seq ^ jnp.where(rep == 0, first, second)
         target = lax.rem(group // per_wid - wid + wid_count, wid_count)
         placed[target, lax.rem(group, per_wid)] = result[shift * sequences : (shift + 1) * sequences]
     for target, out in enumerate(outs):
@@ -373,8 +393,14 @@
     return lax.ppermute(value, axis, [(i, (i + shift) % count) for i in range(count)])
 
 
-def swapped(value, axis, step):
-    return lax.ppermute(value, axis, [(i, i ^ step) for i in range(lax.axis_size(axis))])
+def exchanged(value, steps):
+    cores = lax.axis_size("rep")
+    pairs = [
+        (seq * cores + core, (seq ^ steps[core]) * cores + core)
+        for seq in range(lax.axis_size("seq"))
+        for core in range(cores)
+    ]
+    return lax.ppermute(value, ("seq", "rep"), pairs)
 
 
 def shards(
@@ -398,13 +424,16 @@
     sent, *held = project_other(indices, exponents, blocks, values)
     other = shifted(sent, "rep", 1)
     own = project_own(*held)
+    fisher, own = lax.optimization_barrier((fisher_inverse, own))
+    halves = split_fisher(fisher)
+    own, other, *halves = lax.optimization_barrier((own, other, *halves))
     messages = make_messages(own, other, wid_count)
-    fisher_inverse, *messages = lax.optimization_barrier((fisher_inverse, *messages))
+    fisher, *messages = lax.optimization_barrier((fisher, *messages))
     received = [shifted(m, "wid", shift) for shift, m in enumerate(messages, 1)]
-    high, low = split_fisher(fisher_inverse)
+    high, low = split_fisher(fisher, *halves)
     own, high, low = lax.optimization_barrier((own, high, low))
     outer = outer_products(own, other, received)
-    gathered = [outer] + [swapped(outer, "seq", step) for step in range(1, seq_count)]
+    gathered = [outer] + [exchanged(outer, steps) for steps in exchange_steps(seq_count)]
     parts = fisher_product(gathered, high, low, wid_count)
     result = parts[0]
     for shift in range(1, wid_count):

time: 29.3 us -> 28.7 us (0.980)
  waiting for transfers between devices: 9.69 us -> 8.73 us
    ppermute x3, waiting for transfers between devices: 5.04 us -> 3.72 us  [shifted(): lax.ppermute(value, axis, [(i, (i + shift) % count) for i in range(count)])]
    ppermute x3, waiting for transfers between devices: 4.66 us -> 5.02 us  [exchanged(): return lax.ppermute(value, ('seq', 'rep'), pairs)]
    pallas_call x1 -> x2, Pallas kernels: 3.64 us -> 3.72 us  [split_fisher(): pl.pallas_call(split_late_kernel if halves else split_early_kernel, out_s...]
  transfers between devices with their start and end apart: 6 -> 6, of which waited for: 5 -> 4; matrix products, arithmetic and copies ran while one was open for 0% -> 0% of each run, Pallas kernels for 14% -> 15%
where the time goes in v4:
time: 28.7 us; the launch traced here: 28.6 us
  starting transfers between devices  9.82 us (34%)
  Pallas kernels  9.26 us (32%)
  waiting for transfers between devices  8.73 us (30%)
  other arithmetic  0.7 us (2%)
    ppermute x3, waiting for transfers between devices, exchanged(): return lax.ppermute(value, ('seq', 'rep'), pairs)  5.02 us
    ppermute x3, starting transfers between devices, shifted(): lax.ppermute(value, axis, [(i, (i + shift) % count) for i in range(count)])  5 us
    ppermute x3, starting transfers between devices, exchanged(): return lax.ppermute(value, ('seq', 'rep'), pairs)  4.82 us
    pallas_call x2, Pallas kernels, split_fisher(): pl.pallas_call(split_late_kernel if halves else split_early_kernel, out_s...  3.72 us
    ppermute x3, waiting for transfers between devices, shifted(): lax.ppermute(value, axis, [(i, (i + shift) % count) for i in range(count)])  3.72 us
    pallas_call x1, Pallas kernels, project_other(): pl.pallas_call(project_other_kernel, out_shape=(jax.ShapeDtypeStruct((2 *...  2.64 us
    pallas_call x1, Pallas kernels, fisher_product(): pl.pallas_call(functools.partial(fisher_kernel, wid_count), out_shape=[sh...  2.12 us
    add x1, other arithmetic, shards(): result = result + shifted(parts[shift], 'wid', shift)  0.7 us
  transfers between devices with their start and end apart: 6, of which 4 were waited for; matrix products, arithmetic and copies ran while one was open for 0% of the time, Pallas kernels for 15%

profile of v4, /device:TPU:0, one launch (start us, length us, event | category | flops | bytes accessed | tf_op | source)
XLA Modules:
  0.0 28.6 jit_solution(15329660591001081167)
XLA Ops:
  0.0 2.6 %project_other.1 = (f32[128,512]{1,0:T(8,128)S(1)}, bf16[2,4,8,64,128]{4,3,2,1,0:T(8,128)(2,1)S(1)}, bf16[2,4,8,16,128]{4,3,2,1,0:T(8,128)(2,1)S(1)}, bf16[2,4,64,128]{3,2,1,0:T(8,128)(2,1)S(1)}) custom-call(s32[4]{0:T(128)} %act_index.1, s32[4]{0:T(128)} %grad_index.1, s32[16,16]{1,0:T(8,128)} %act_exponents.1, s32[16,16]{1,0:T(8,128)} %grad_exponents.1, ...), custom_call_target="tpu_custom_call" | custom-call | flops 67108864 | bytes 2359296 | tf_op jit(solution)/shard_map/project_other/pallas_call | solution.py:137
  2.6 0.5 %collective-permute-start = (f32[128,512]{1,0:T(8,128)S(1)}, f32[128,512]{1,0:T(8,128)S(1)}, u32[]{:S(2)}, u32[]{:S(2)}) collective-permute-start(f32[128,512]{1,0:T(8,128)S(1)} %get-tuple-element.30), channel_id=1, source_target_pairs={{0,1},{1,0},{2,3},{3,2},{4,5},{5,4},{6,7},{7,6},{8,9},{9,8},{10,11... | collective-permute-start | bytes 786440 | tf_op jit(solution)/shard_map/ppermute | solution.py:393
  3.2 0.4 %project_own.1.own = f32[128,512]{1,0:T(8,128)S(1)} custom-call(bf16[2,4,8,64,128]{4,3,2,1,0:T(8,128)(2,1)S(1)} %get-tuple-element.26.picked, bf16[2,4,8,16,128]{4,3,2,1,0:T(8,128)(2,1)S(1)} %get-tuple-element.27.scales, bf16[2,4,64,128]{3,2,1,0:T(8,128)(2,1)S(1)} %get-tuple-element.28.weights), custom_call_target="tpu_custom_call" | custom-call | flops 67108864 | bytes 1310720 | tf_op jit(solution)/shard_map/project_own/pallas_call | solution.py:176
  3.6 0.1 split_early.1
  3.7 0.6 %collective-permute-done.other = f32[128,512]{1,0:T(8,128)S(1)} collective-permute-done((f32[128,512]{1,0:T(8,128)S(1)}, f32[128,512]{1,0:T(8,128)S(1)}, u32[]{:S(2)}, u32[]{:S(2)}) %collective-permute-start) | collective-permute-done | bytes 262176 | tf_op jit(solution)/shard_map/ppermute | solution.py:393
  4.4 2.9 %collective-permute-start.1 = (f32[96,512]{1,0:T(8,128)S(1)}, f32[96,512]{1,0:T(8,128)S(1)}, u32[]{:S(2)}, u32[]{:S(2)}) collective-permute-start(f32[96,512]{1,0:T(8,128)S(1)} %make_messages.1), channel_id=1, source_target_pairs={{0,2},{2,0},{1,3},{3,1},{4,6},{6,4},{5,7},{7,5},{8,10},{10,8},{9,1... | collective-permute-start | bytes 589832 | tf_op jit(solution)/shard_map/ppermute | solution.py:393
  7.3 3.6 %split_late.1 = (bf16[1024,2048]{1,0:T(8,128)(2,1)S(1)}, bf16[1024,2048]{1,0:T(8,128)(2,1)S(1)}) custom-call(f32[1024,2048]{1,0:T(8,128)} %fisher.1, bf16[1024,2048]{1,0:T(8,128)(2,1)S(1)} %get-tuple-element.37.high_in, bf16[1024,2048]{1,0:T(8,128)(2,1)S(1)} %get-tuple-element.38.low_in), custom_call_target="tpu_custom_call", output_to_operand_aliasing={{0}: (1, {}), {1}: (2, {})} | custom-call | flops 4194304 | bytes 16777216 | tf_op jit(solution)/shard_map/split_late/pallas_call | solution.py:227
  10.9 0.0 collective-permute-done.1.rest_0_
  10.9 0.3 %outer_products.1.refs_0_ = f32[128,128]{1,0:T(8,128)S(1)} custom-call(f32[128,512]{1,0:T(8,128)S(1)} %project_own.1.own, f32[128,512]{1,0:T(8,128)S(1)} %collective-permute-done.other, f32[96,512]{1,0:T(8,128)S(1)} %collective-permute-done.1.rest_0_), custom_call_target="tpu_custom_call" | custom-call | tf_op jit(solution)/shard_map/outer_products/pallas_call | solution.py:303
  11.3 4.2 %collective-permute-start.4 = (f32[128,128]{1,0:T(8,128)S(1)}, f32[128,128]{1,0:T(8,128)S(1)}, u32[]{:S(2)}, u32[]{:S(2)}) collective-permute-start(f32[128,128]{1,0:T(8,128)S(1)} %outer_products.1.refs_0_), channel_id=1, source_target_pairs={{0,12},{1,13},{4,8},{5,9},{8,4},{9,5},{12,0},{13,1},{2,14},{3,15},... | collective-permute-start | bytes 196616 | tf_op jit(solution)/shard_map/ppermute | solution.py:403
  15.4 0.0 collective-permute-start.3
  15.4 0.6 %collective-permute-start.2 = (f32[128,128]{1,0:T(8,128)S(1)}, f32[128,128]{1,0:T(8,128)S(1)}, u32[]{:S(2)}, u32[]{:S(2)}) collective-permute-start(f32[128,128]{1,0:T(8,128)S(1)} %outer_products.1.refs_0_), channel_id=1, source_target_pairs={{0,4},{1,9},{4,0},{5,13},{8,12},{9,1},{12,8},{13,5},{2,6},{3,11},{... | collective-permute-start | bytes 196616 | tf_op jit(solution)/shard_map/ppermute | solution.py:403
  16.1 1.7 %collective-permute-done.4.refs_3_ = f32[128,128]{1,0:T(8,128)S(1)} collective-permute-done((f32[128,128]{1,0:T(8,128)S(1)}, f32[128,128]{1,0:T(8,128)S(1)}, u32[]{:S(2)}, u32[]{:S(2)}) %collective-permute-start.4) | collective-permute-done | bytes 65568 | tf_op jit(solution)/shard_map/ppermute | solution.py:403
  17.8 3.3 %collective-permute-done.3.refs_2_ = f32[128,128]{1,0:T(8,128)S(1)} collective-permute-done((f32[128,128]{1,0:T(8,128)S(1)}, f32[128,128]{1,0:T(8,128)S(1)}, u32[]{:S(2)}, u32[]{:S(2)}) %collective-permute-start.3) | collective-permute-done | bytes 65568 | tf_op jit(solution)/shard_map/ppermute | solution.py:403
  21.1 0.0 collective-permute-done.2.refs_1_
  21.1 2.1 %fisher_product.1 = (f32[16,1,1024]{2,1,0:T(1,128)S(1)}, f32[16,1,1024]{2,1,0:T(1,128)S(1)}) custom-call(f32[128,128]{1,0:T(8,128)S(1)} %outer_products.1.refs_0_, f32[128,128]{1,0:T(8,128)S(1)} %collective-permute-done.2.refs_1_, f32[128,128]{1,0:T(8,128)S(1)} %collective-permute-done.3.refs_2_, f32[128,128]{1,0:T(8,128)S(1)} %collective-permute-done.4.refs_3_, ...), custom_call_target="tpu_custom_call" | custom-call | tf_op jit(solution)/shard_map/fisher_product/pallas_call | solution.py:380
  23.2 1.6 %collective-permute-start.5 = (f32[16,1,1024]{2,1,0:T(1,128)S(1)}, f32[16,1,1024]{2,1,0:T(1,128)S(1)}, u32[]{:S(2)}, u32[]{:S(2)}) collective-permute-start(f32[16,1,1024]{2,1,0:T(1,128)S(1)} %get-tuple-element.46), channel_id=1, source_target_pairs={{0,2},{2,0},{1,3},{3,1},{4,6},{6,4},{5,7},{7,5},{8,10},{10,8},{9,1... | collective-permute-start | bytes 196616 | tf_op jit(solution)/shard_map/ppermute | solution.py:393
  24.8 3.1 %collective-permute-done.5 = f32[16,1,1024]{2,1,0:T(1,128)S(1)} collective-permute-done((f32[16,1,1024]{2,1,0:T(1,128)S(1)}, f32[16,1,1024]{2,1,0:T(1,128)S(1)}, u32[]{:S(2)}, u32[]{:S(2)}) %collective-permute-start.5) | collective-permute-done | bytes 65568 | tf_op jit(solution)/shard_map/ppermute | solution.py:393
  27.9 0.7 %add.3 = f32[16,1,1024]{2,1,0:T(1,128)} add(f32[16,1,1024]{2,1,0:T(1,128)S(1)} %get-tuple-element.45, f32[16,1,1024]{2,1,0:T(1,128)S(1)} %collective-permute-done.5) | non-fusion elementwise | flops 16384 | bytes 196608 | tf_op jit(solution)/shard_map/add | solution.py:440
  (1 shorter events, 0.0 us)
Async XLA Ops:
  2.6 1.7 %collective-permute-start = (f32[128,512]{1,0:T(8,128)S(1)}, f32[128,512]{1,0:T(8,128)S(1)}, u32[]{:S(2)}, u32[]{:S(2)}) collective-permute-start(f32[128,512]{1,0:T(8,128)S(1)} %get-tuple-element.30), channel_id=1, source_target_pairs={{0,1},{1,0},{2,3},{3,2},{4,5},{5,4},{6,7},{7,6},{8,9},{9,8},{10,11... | collective-permute-start | bytes 786440 | tf_op jit(solution)/shard_map/ppermute | solution.py:393
  4.4 6.6 %collective-permute-start.1 = (f32[96,512]{1,0:T(8,128)S(1)}, f32[96,512]{1,0:T(8,128)S(1)}, u32[]{:S(2)}, u32[]{:S(2)}) collective-permute-start(f32[96,512]{1,0:T(8,128)S(1)} %make_messages.1), channel_id=1, source_target_pairs={{0,2},{2,0},{1,3},{3,1},{4,6},{6,4},{5,7},{7,5},{8,10},{10,8},{9,1... | collective-permute-start | bytes 589832 | tf_op jit(solution)/shard_map/ppermute | solution.py:393
  11.3 6.5 %collective-permute-start.4 = (f32[128,128]{1,0:T(8,128)S(1)}, f32[128,128]{1,0:T(8,128)S(1)}, u32[]{:S(2)}, u32[]{:S(2)}) collective-permute-start(f32[128,128]{1,0:T(8,128)S(1)} %outer_products.1.refs_0_), channel_id=1, source_target_pairs={{0,12},{1,13},{4,8},{5,9},{8,4},{9,5},{12,0},{13,1},{2,14},{3,15},... | collective-permute-start | bytes 196616 | tf_op jit(solution)/shard_map/ppermute | solution.py:403
  15.4 5.7 %collective-permute-start.3 = (f32[128,128]{1,0:T(8,128)S(1)}, f32[128,128]{1,0:T(8,128)S(1)}, u32[]{:S(2)}, u32[]{:S(2)}) collective-permute-start(f32[128,128]{1,0:T(8,128)S(1)} %outer_products.1.refs_0_), channel_id=1, source_target_pairs={{0,8},{1,5},{4,12},{5,1},{8,0},{9,13},{12,4},{13,9},{2,10},{3,7},{... | collective-permute-start | bytes 196616 | tf_op jit(solution)/shard_map/ppermute | solution.py:403
  15.4 5.7 %collective-permute-start.2 = (f32[128,128]{1,0:T(8,128)S(1)}, f32[128,128]{1,0:T(8,128)S(1)}, u32[]{:S(2)}, u32[]{:S(2)}) collective-permute-start(f32[128,128]{1,0:T(8,128)S(1)} %outer_products.1.refs_0_), channel_id=1, source_target_pairs={{0,4},{1,9},{4,0},{5,13},{8,12},{9,1},{12,8},{13,5},{2,6},{3,11},{... | collective-permute-start | bytes 196616 | tf_op jit(solution)/shard_map/ppermute | solution.py:403
  23.2 4.6 %collective-permute-start.5 = (f32[16,1,1024]{2,1,0:T(1,128)S(1)}, f32[16,1,1024]{2,1,0:T(1,128)S(1)}, u32[]{:S(2)}, u32[]{:S(2)}) collective-permute-start(f32[16,1,1024]{2,1,0:T(1,128)S(1)} %get-tuple-element.46), channel_id=1, source_target_pairs={{0,2},{2,0},{1,3},{3,1},{4,6},{6,4},{5,7},{7,5},{8,10},{10,8},{9,1... | collective-permute-start | bytes 196616 | tf_op jit(solution)/shard_map/ppermute | solution.py:393

commit v5 on v4

--- a/solution.py
+++ b/solution.py
@@ -214,11 +214,19 @@
 
 
 def split_late_kernel(fisher, high_in, low_in, high, low, held, sems):
-    del high_in, low_in
-
-    @pl.when(lax.axis_index("rep") == 0)
+    first_core = lax.axis_index("rep") == 0
+
+    @pl.when(first_core)
     def _():
         split_pieces(fisher, high, low, held, sems)
+
+    @pl.when(~first_core)
+    def _():
+        @pl.loop(0, high.shape[0] // 16)
+        def _(step):
+            rows = pl.ds(pl.multiple_of(step * 16, 16), 16)
+            high[rows, :] = high_in[rows, :]
+            low[rows, :] = low_in[rows, :]
 
 
 def split_fisher(fisher, *halves):
@@ -233,7 +241,6 @@
             pltpu.VMEM((PIECES, rows // PIECES, columns), F32),
             pltpu.SemaphoreType.DMA((PIECES,)),
         ],
-        input_output_aliases={1: 0, 2: 1} if halves else {},
         cost_estimate=pl.CostEstimate(
             flops=2 * rows * columns, bytes_accessed=8 * rows * columns, transcendentals=0
         ),

time: 28.7 us -> 28.7 us (level)
  no operation moved by 1% of the time
where the time goes in v5:
time: 28.7 us; the launch traced here: 28.6 us
  starting transfers between devices  9.81 us (34%)
  Pallas kernels  9.27 us (32%)
  waiting for transfers between devices  8.73 us (30%)
  other arithmetic  0.7 us (2%)
    ppermute x3, waiting for transfers between devices, exchanged(): return lax.ppermute(value, ('seq', 'rep'), pairs)  5.02 us
    ppermute x3, starting transfers between devices, shifted(): lax.ppermute(value, axis, [(i, (i + shift) % count) for i in range(count)])  5 us
    ppermute x3, starting transfers between devices, exchanged(): return lax.ppermute(value, ('seq', 'rep'), pairs)  4.81 us
    pallas_call x2, Pallas kernels, split_fisher(): pl.pallas_call(split_late_kernel if halves else split_early_kernel, out_s...  3.72 us
    ppermute x3, waiting for transfers between devices, shifted(): lax.ppermute(value, axis, [(i, (i + shift) % count) for i in range(count)])  3.72 us
    pallas_call x1, Pallas kernels, project_other(): pl.pallas_call(project_other_kernel, out_shape=(jax.ShapeDtypeStruct((2 *...  2.64 us
    pallas_call x1, Pallas kernels, fisher_product(): pl.pallas_call(functools.partial(fisher_kernel, wid_count), out_shape=[sh...  2.12 us
    add x1, other arithmetic, shards(): result = result + shifted(parts[shift], 'wid', shift)  0.7 us
  transfers between devices with their start and end apart: 6, of which 4 were waited for; matrix products, arithmetic and copies ran while one was open for 0% of the time, Pallas kernels for 15%

profile of v5, /device:TPU:0, one launch (start us, length us, event | category | flops | bytes accessed | tf_op | source)
XLA Modules:
  0.0 28.6 jit_solution(10196734210754053300)
XLA Ops:
  0.0 2.6 %project_other.1 = (f32[128,512]{1,0:T(8,128)S(1)}, bf16[2,4,8,64,128]{4,3,2,1,0:T(8,128)(2,1)S(1)}, bf16[2,4,8,16,128]{4,3,2,1,0:T(8,128)(2,1)S(1)}, bf16[2,4,64,128]{3,2,1,0:T(8,128)(2,1)S(1)}) custom-call(s32[4]{0:T(128)} %act_index.1, s32[4]{0:T(128)} %grad_index.1, s32[16,16]{1,0:T(8,128)} %act_exponents.1, s32[16,16]{1,0:T(8,128)} %grad_exponents.1, ...), custom_call_target="tpu_custom_call" | custom-call | flops 67108864 | bytes 2359296 | tf_op jit(solution)/shard_map/project_other/pallas_call | solution.py:137
  2.6 0.5 %collective-permute-start = (f32[128,512]{1,0:T(8,128)S(1)}, f32[128,512]{1,0:T(8,128)S(1)}, u32[]{:S(2)}, u32[]{:S(2)}) collective-permute-start(f32[128,512]{1,0:T(8,128)S(1)} %get-tuple-element.30), channel_id=1, source_target_pairs={{0,1},{1,0},{2,3},{3,2},{4,5},{5,4},{6,7},{7,6},{8,9},{9,8},{10,11... | collective-permute-start | bytes 786440 | tf_op jit(solution)/shard_map/ppermute | solution.py:400
  3.2 0.4 %project_own.1.own = f32[128,512]{1,0:T(8,128)S(1)} custom-call(bf16[2,4,8,64,128]{4,3,2,1,0:T(8,128)(2,1)S(1)} %get-tuple-element.26.picked, bf16[2,4,8,16,128]{4,3,2,1,0:T(8,128)(2,1)S(1)} %get-tuple-element.27.scales, bf16[2,4,64,128]{3,2,1,0:T(8,128)(2,1)S(1)} %get-tuple-element.28.weights), custom_call_target="tpu_custom_call" | custom-call | flops 67108864 | bytes 1310720 | tf_op jit(solution)/shard_map/project_own/pallas_call | solution.py:176
  3.6 0.1 split_early.1
  3.7 0.6 %collective-permute-done.other = f32[128,512]{1,0:T(8,128)S(1)} collective-permute-done((f32[128,512]{1,0:T(8,128)S(1)}, f32[128,512]{1,0:T(8,128)S(1)}, u32[]{:S(2)}, u32[]{:S(2)}) %collective-permute-start) | collective-permute-done | bytes 262176 | tf_op jit(solution)/shard_map/ppermute | solution.py:400
  4.4 2.9 %collective-permute-start.1 = (f32[96,512]{1,0:T(8,128)S(1)}, f32[96,512]{1,0:T(8,128)S(1)}, u32[]{:S(2)}, u32[]{:S(2)}) collective-permute-start(f32[96,512]{1,0:T(8,128)S(1)} %make_messages.1), channel_id=1, source_target_pairs={{0,2},{2,0},{1,3},{3,1},{4,6},{6,4},{5,7},{7,5},{8,10},{10,8},{9,1... | collective-permute-start | bytes 589832 | tf_op jit(solution)/shard_map/ppermute | solution.py:400
  7.3 3.6 %split_late.1 = (bf16[1024,2048]{1,0:T(8,128)(2,1)S(1)}, bf16[1024,2048]{1,0:T(8,128)(2,1)S(1)}) custom-call(f32[1024,2048]{1,0:T(8,128)} %fisher.1, bf16[1024,2048]{1,0:T(8,128)(2,1)S(1)} %get-tuple-element.37.high_in, bf16[1024,2048]{1,0:T(8,128)(2,1)S(1)} %get-tuple-element.38.low_in), custom_call_target="tpu_custom_call" | custom-call | flops 4194304 | bytes 16777216 | tf_op jit(solution)/shard_map/split_late/pallas_call | solution.py:235
  10.9 0.0 collective-permute-done.1.rest_0_
  10.9 0.3 %outer_products.1.refs_0_ = f32[128,128]{1,0:T(8,128)S(1)} custom-call(f32[128,512]{1,0:T(8,128)S(1)} %project_own.1.own, f32[128,512]{1,0:T(8,128)S(1)} %collective-permute-done.other, f32[96,512]{1,0:T(8,128)S(1)} %collective-permute-done.1.rest_0_), custom_call_target="tpu_custom_call" | custom-call | tf_op jit(solution)/shard_map/outer_products/pallas_call | solution.py:310
  11.3 4.2 %collective-permute-start.4 = (f32[128,128]{1,0:T(8,128)S(1)}, f32[128,128]{1,0:T(8,128)S(1)}, u32[]{:S(2)}, u32[]{:S(2)}) collective-permute-start(f32[128,128]{1,0:T(8,128)S(1)} %outer_products.1.refs_0_), channel_id=1, source_target_pairs={{0,12},{1,13},{4,8},{5,9},{8,4},{9,5},{12,0},{13,1},{2,14},{3,15},... | collective-permute-start | bytes 196616 | tf_op jit(solution)/shard_map/ppermute | solution.py:410
  15.4 0.0 collective-permute-start.3
  15.4 0.6 %collective-permute-start.2 = (f32[128,128]{1,0:T(8,128)S(1)}, f32[128,128]{1,0:T(8,128)S(1)}, u32[]{:S(2)}, u32[]{:S(2)}) collective-permute-start(f32[128,128]{1,0:T(8,128)S(1)} %outer_products.1.refs_0_), channel_id=1, source_target_pairs={{0,4},{1,9},{4,0},{5,13},{8,12},{9,1},{12,8},{13,5},{2,6},{3,11},{... | collective-permute-start | bytes 196616 | tf_op jit(solution)/shard_map/ppermute | solution.py:410
  16.1 1.7 %collective-permute-done.4.refs_3_ = f32[128,128]{1,0:T(8,128)S(1)} collective-permute-done((f32[128,128]{1,0:T(8,128)S(1)}, f32[128,128]{1,0:T(8,128)S(1)}, u32[]{:S(2)}, u32[]{:S(2)}) %collective-permute-start.4) | collective-permute-done | bytes 65568 | tf_op jit(solution)/shard_map/ppermute | solution.py:410
  17.8 3.3 %collective-permute-done.3.refs_2_ = f32[128,128]{1,0:T(8,128)S(1)} collective-permute-done((f32[128,128]{1,0:T(8,128)S(1)}, f32[128,128]{1,0:T(8,128)S(1)}, u32[]{:S(2)}, u32[]{:S(2)}) %collective-permute-start.3) | collective-permute-done | bytes 65568 | tf_op jit(solution)/shard_map/ppermute | solution.py:410
  21.1 0.0 collective-permute-done.2.refs_1_
  21.1 2.1 %fisher_product.1 = (f32[16,1,1024]{2,1,0:T(1,128)S(1)}, f32[16,1,1024]{2,1,0:T(1,128)S(1)}) custom-call(f32[128,128]{1,0:T(8,128)S(1)} %outer_products.1.refs_0_, f32[128,128]{1,0:T(8,128)S(1)} %collective-permute-done.2.refs_1_, f32[128,128]{1,0:T(8,128)S(1)} %collective-permute-done.3.refs_2_, f32[128,128]{1,0:T(8,128)S(1)} %collective-permute-done.4.refs_3_, ...), custom_call_target="tpu_custom_call" | custom-call | tf_op jit(solution)/shard_map/fisher_product/pallas_call | solution.py:387
  23.2 1.6 %collective-permute-start.5 = (f32[16,1,1024]{2,1,0:T(1,128)S(1)}, f32[16,1,1024]{2,1,0:T(1,128)S(1)}, u32[]{:S(2)}, u32[]{:S(2)}) collective-permute-start(f32[16,1,1024]{2,1,0:T(1,128)S(1)} %get-tuple-element.46), channel_id=1, source_target_pairs={{0,2},{2,0},{1,3},{3,1},{4,6},{6,4},{5,7},{7,5},{8,10},{10,8},{9,1... | collective-permute-start | bytes 196616 | tf_op jit(solution)/shard_map/ppermute | solution.py:400
  24.8 3.1 %collective-permute-done.5 = f32[16,1,1024]{2,1,0:T(1,128)S(1)} collective-permute-done((f32[16,1,1024]{2,1,0:T(1,128)S(1)}, f32[16,1,1024]{2,1,0:T(1,128)S(1)}, u32[]{:S(2)}, u32[]{:S(2)}) %collective-permute-start.5) | collective-permute-done | bytes 65568 | tf_op jit(solution)/shard_map/ppermute | solution.py:400
  27.9 0.7 %add.3 = f32[16,1,1024]{2,1,0:T(1,128)} add(f32[16,1,1024]{2,1,0:T(1,128)S(1)} %get-tuple-element.45, f32[16,1,1024]{2,1,0:T(1,128)S(1)} %collective-permute-done.5) | non-fusion elementwise | flops 16384 | bytes 196608 | tf_op jit(solution)/shard_map/add | solution.py:447
  (1 shorter events, 0.0 us)
Async XLA Ops:
  2.6 1.7 %collective-permute-start = (f32[128,512]{1,0:T(8,128)S(1)}, f32[128,512]{1,0:T(8,128)S(1)}, u32[]{:S(2)}, u32[]{:S(2)}) collective-permute-start(f32[128,512]{1,0:T(8,128)S(1)} %get-tuple-element.30), channel_id=1, source_target_pairs={{0,1},{1,0},{2,3},{3,2},{4,5},{5,4},{6,7},{7,6},{8,9},{9,8},{10,11... | collective-permute-start | bytes 786440 | tf_op jit(solution)/shard_map/ppermute | solution.py:400
  4.4 6.6 %collective-permute-start.1 = (f32[96,512]{1,0:T(8,128)S(1)}, f32[96,512]{1,0:T(8,128)S(1)}, u32[]{:S(2)}, u32[]{:S(2)}) collective-permute-start(f32[96,512]{1,0:T(8,128)S(1)} %make_messages.1), channel_id=1, source_target_pairs={{0,2},{2,0},{1,3},{3,1},{4,6},{6,4},{5,7},{7,5},{8,10},{10,8},{9,1... | collective-permute-start | bytes 589832 | tf_op jit(solution)/shard_map/ppermute | solution.py:400
  11.3 6.5 %collective-permute-start.4 = (f32[128,128]{1,0:T(8,128)S(1)}, f32[128,128]{1,0:T(8,128)S(1)}, u32[]{:S(2)}, u32[]{:S(2)}) collective-permute-start(f32[128,128]{1,0:T(8,128)S(1)} %outer_products.1.refs_0_), channel_id=1, source_target_pairs={{0,12},{1,13},{4,8},{5,9},{8,4},{9,5},{12,0},{13,1},{2,14},{3,15},... | collective-permute-start | bytes 196616 | tf_op jit(solution)/shard_map/ppermute | solution.py:410
  15.4 5.7 %collective-permute-start.3 = (f32[128,128]{1,0:T(8,128)S(1)}, f32[128,128]{1,0:T(8,128)S(1)}, u32[]{:S(2)}, u32[]{:S(2)}) collective-permute-start(f32[128,128]{1,0:T(8,128)S(1)} %outer_products.1.refs_0_), channel_id=1, source_target_pairs={{0,8},{1,5},{4,12},{5,1},{8,0},{9,13},{12,4},{13,9},{2,10},{3,7},{... | collective-permute-start | bytes 196616 | tf_op jit(solution)/shard_map/ppermute | solution.py:410
  15.4 5.7 %collective-permute-start.2 = (f32[128,128]{1,0:T(8,128)S(1)}, f32[128,128]{1,0:T(8,128)S(1)}, u32[]{:S(2)}, u32[]{:S(2)}) collective-permute-start(f32[128,128]{1,0:T(8,128)S(1)} %outer_products.1.refs_0_), channel_id=1, source_target_pairs={{0,4},{1,9},{4,0},{5,13},{8,12},{9,1},{12,8},{13,5},{2,6},{3,11},{... | collective-permute-start | bytes 196616 | tf_op jit(solution)/shard_map/ppermute | solution.py:410
  23.2 4.6 %collective-permute-start.5 = (f32[16,1,1024]{2,1,0:T(1,128)S(1)}, f32[16,1,1024]{2,1,0:T(1,128)S(1)}, u32[]{:S(2)}, u32[]{:S(2)}) collective-permute-start(f32[16,1,1024]{2,1,0:T(1,128)S(1)} %get-tuple-element.46), channel_id=1, source_target_pairs={{0,2},{2,0},{1,3},{3,1},{4,6},{6,4},{5,7},{7,5},{8,10},{10,8},{9,1... | collective-permute-start | bytes 196616 | tf_op jit(solution)/shard_map/ppermute | solution.py:400

commit v6 on v5

--- a/solution.py
+++ b/solution.py
@@ -28,7 +28,9 @@
     left_high, left_low = two_parts(left)
     right_high, right_low = two_parts(right)
     dot = functools.partial(lax.dot_general, dimension_numbers=dims, preferred_element_type=F32)
-    return dot(left_high, right_high) + (dot(left_high, right_low) + dot(left_low, right_high))
+    rows = left.shape[0]
+    main = dot(jnp.concatenate([left_high, left_low], axis=0), right_high)
+    return main[:rows] + (main[rows:] + dot(left_high, right_low))
 
 
 def scaled_rows(rows, scale):
@@ -288,15 +290,17 @@
     pairs = acts.shape[1] // BLK
     lane = lax.broadcasted_iota(jnp.int32, (half, BLK), 1)
     for pair in range(pairs):
-        columns = slice(pair * BLK, (pair + 1) * BLK)
-        staged[pair] = grads[:, columns]
+        staged[pair] = grads[:, pair * BLK : (pair + 1) * BLK]
+    results = []
+    for pair in range(pairs):
         pieces = []
         for odd in range(2):
             part = staged[pair, pl.ds(odd, half, stride=2), :]
             pieces.append(jnp.where(lane < LEN, part, 0.0))
             pieces.append(jnp.where(lane < LEN, 0.0, part))
         left = jnp.concatenate(pieces, axis=0)
-        result = product(left, acts[:, columns], NT) * (1.0 / LEN)
+        results.append(product(left, acts[:, pair * BLK : (pair + 1) * BLK], NT) * (1.0 / LEN))
+    for pair, result in enumerate(results):
         both = jnp.concatenate([result[: 2 * half, :], result[2 * half :, :]], axis=1)
         out[pl.ds(2 * pair, half, stride=2 * pairs), :] = both[:half, :]
         out[pl.ds(2 * pair + 1, half, stride=2 * pairs), :] = both[half:, :]

time: 28.7 us -> 28.7 us (level)
  no operation moved by 1% of the time
where the time goes in v6:
time: 28.7 us; the launch traced here: 28.5 us
  starting transfers between devices  9.82 us (34%)
  Pallas kernels  9.23 us (32%)
  waiting for transfers between devices  8.73 us (30%)
  other arithmetic  0.7 us (2%)
    ppermute x3, waiting for transfers between devices, exchanged(): return lax.ppermute(value, ('seq', 'rep'), pairs)  5.02 us
    ppermute x3, starting transfers between devices, shifted(): lax.ppermute(value, axis, [(i, (i + shift) % count) for i in range(count)])  5 us
    ppermute x3, starting transfers between devices, exchanged(): return lax.ppermute(value, ('seq', 'rep'), pairs)  4.83 us
    pallas_call x2, Pallas kernels, split_fisher(): pl.pallas_call(split_late_kernel if halves else split_early_kernel, out_s...  3.72 us
    ppermute x3, waiting for transfers between devices, shifted(): lax.ppermute(value, axis, [(i, (i + shift) % count) for i in range(count)])  3.72 us
    pallas_call x1, Pallas kernels, project_other(): pl.pallas_call(project_other_kernel, out_shape=(jax.ShapeDtypeStruct((2 *...  2.64 us
    pallas_call x1, Pallas kernels, fisher_product(): pl.pallas_call(functools.partial(fisher_kernel, wid_count), out_shape=[sh...  2.12 us
    add x1, other arithmetic, shards(): result = result + shifted(parts[shift], 'wid', shift)  0.7 us
  transfers between devices with their start and end apart: 6, of which 4 were waited for; matrix products, arithmetic and copies ran while one was open for 0% of the time, Pallas kernels for 15%

profile of v6, /device:TPU:0, one launch (start us, length us, event | category | flops | bytes accessed | tf_op | source)
XLA Modules:
  0.0 28.5 jit_solution(14195837052764564337)
XLA Ops:
  0.0 2.6 %project_other.1 = (f32[128,512]{1,0:T(8,128)S(1)}, bf16[2,4,8,64,128]{4,3,2,1,0:T(8,128)(2,1)S(1)}, bf16[2,4,8,16,128]{4,3,2,1,0:T(8,128)(2,1)S(1)}, bf16[2,4,64,128]{3,2,1,0:T(8,128)(2,1)S(1)}) custom-call(s32[4]{0:T(128)} %act_index.1, s32[4]{0:T(128)} %grad_index.1, s32[16,16]{1,0:T(8,128)} %act_exponents.1, s32[16,16]{1,0:T(8,128)} %grad_exponents.1, ...), custom_call_target="tpu_custom_call" | custom-call | flops 67108864 | bytes 2359296 | tf_op jit(solution)/shard_map/project_other/pallas_call | solution.py:139
  2.6 0.5 %collective-permute-start = (f32[128,512]{1,0:T(8,128)S(1)}, f32[128,512]{1,0:T(8,128)S(1)}, u32[]{:S(2)}, u32[]{:S(2)}) collective-permute-start(f32[128,512]{1,0:T(8,128)S(1)} %get-tuple-element.30), channel_id=1, source_target_pairs={{0,1},{1,0},{2,3},{3,2},{4,5},{5,4},{6,7},{7,6},{8,9},{9,8},{10,11... | collective-permute-start | bytes 786440 | tf_op jit(solution)/shard_map/ppermute | solution.py:404
  3.2 0.4 %project_own.1.own = f32[128,512]{1,0:T(8,128)S(1)} custom-call(bf16[2,4,8,64,128]{4,3,2,1,0:T(8,128)(2,1)S(1)} %get-tuple-element.26.picked, bf16[2,4,8,16,128]{4,3,2,1,0:T(8,128)(2,1)S(1)} %get-tuple-element.27.scales, bf16[2,4,64,128]{3,2,1,0:T(8,128)(2,1)S(1)} %get-tuple-element.28.weights), custom_call_target="tpu_custom_call" | custom-call | flops 67108864 | bytes 1310720 | tf_op jit(solution)/shard_map/project_own/pallas_call | solution.py:178
  3.6 0.1 split_early.1
  3.7 0.6 %collective-permute-done.other = f32[128,512]{1,0:T(8,128)S(1)} collective-permute-done((f32[128,512]{1,0:T(8,128)S(1)}, f32[128,512]{1,0:T(8,128)S(1)}, u32[]{:S(2)}, u32[]{:S(2)}) %collective-permute-start) | collective-permute-done | bytes 262176 | tf_op jit(solution)/shard_map/ppermute | solution.py:404
  4.4 2.9 %collective-permute-start.1 = (f32[96,512]{1,0:T(8,128)S(1)}, f32[96,512]{1,0:T(8,128)S(1)}, u32[]{:S(2)}, u32[]{:S(2)}) collective-permute-start(f32[96,512]{1,0:T(8,128)S(1)} %make_messages.1), channel_id=1, source_target_pairs={{0,2},{2,0},{1,3},{3,1},{4,6},{6,4},{5,7},{7,5},{8,10},{10,8},{9,1... | collective-permute-start | bytes 589832 | tf_op jit(solution)/shard_map/ppermute | solution.py:404
  7.3 3.6 %split_late.1 = (bf16[1024,2048]{1,0:T(8,128)(2,1)S(1)}, bf16[1024,2048]{1,0:T(8,128)(2,1)S(1)}) custom-call(f32[1024,2048]{1,0:T(8,128)} %fisher.1, bf16[1024,2048]{1,0:T(8,128)(2,1)S(1)} %get-tuple-element.37.high_in, bf16[1024,2048]{1,0:T(8,128)(2,1)S(1)} %get-tuple-element.38.low_in), custom_call_target="tpu_custom_call" | custom-call | flops 4194304 | bytes 16777216 | tf_op jit(solution)/shard_map/split_late/pallas_call | solution.py:237
  10.9 0.0 collective-permute-done.1.rest_0_
  10.9 0.3 outer_products.1.refs_0_
  11.2 4.2 %collective-permute-start.4 = (f32[128,128]{1,0:T(8,128)S(1)}, f32[128,128]{1,0:T(8,128)S(1)}, u32[]{:S(2)}, u32[]{:S(2)}) collective-permute-start(f32[128,128]{1,0:T(8,128)S(1)} %outer_products.1.refs_0_), channel_id=1, source_target_pairs={{0,12},{1,13},{4,8},{5,9},{8,4},{9,5},{12,0},{13,1},{2,14},{3,15},... | collective-permute-start | bytes 196616 | tf_op jit(solution)/shard_map/ppermute | solution.py:414
  15.4 0.0 collective-permute-start.3
  15.4 0.6 %collective-permute-start.2 = (f32[128,128]{1,0:T(8,128)S(1)}, f32[128,128]{1,0:T(8,128)S(1)}, u32[]{:S(2)}, u32[]{:S(2)}) collective-permute-start(f32[128,128]{1,0:T(8,128)S(1)} %outer_products.1.refs_0_), channel_id=1, source_target_pairs={{0,4},{1,9},{4,0},{5,13},{8,12},{9,1},{12,8},{13,5},{2,6},{3,11},{... | collective-permute-start | bytes 196616 | tf_op jit(solution)/shard_map/ppermute | solution.py:414
  16.0 1.7 %collective-permute-done.4.refs_3_ = f32[128,128]{1,0:T(8,128)S(1)} collective-permute-done((f32[128,128]{1,0:T(8,128)S(1)}, f32[128,128]{1,0:T(8,128)S(1)}, u32[]{:S(2)}, u32[]{:S(2)}) %collective-permute-start.4) | collective-permute-done | bytes 65568 | tf_op jit(solution)/shard_map/ppermute | solution.py:414
  17.8 3.3 %collective-permute-done.3.refs_2_ = f32[128,128]{1,0:T(8,128)S(1)} collective-permute-done((f32[128,128]{1,0:T(8,128)S(1)}, f32[128,128]{1,0:T(8,128)S(1)}, u32[]{:S(2)}, u32[]{:S(2)}) %collective-permute-start.3) | collective-permute-done | bytes 65568 | tf_op jit(solution)/shard_map/ppermute | solution.py:414
  21.1 0.0 collective-permute-done.2.refs_1_
  21.1 2.1 %fisher_product.1 = (f32[16,1,1024]{2,1,0:T(1,128)S(1)}, f32[16,1,1024]{2,1,0:T(1,128)S(1)}) custom-call(f32[128,128]{1,0:T(8,128)S(1)} %outer_products.1.refs_0_, f32[128,128]{1,0:T(8,128)S(1)} %collective-permute-done.2.refs_1_, f32[128,128]{1,0:T(8,128)S(1)} %collective-permute-done.3.refs_2_, f32[128,128]{1,0:T(8,128)S(1)} %collective-permute-done.4.refs_3_, ...), custom_call_target="tpu_custom_call" | custom-call | tf_op jit(solution)/shard_map/fisher_product/pallas_call | solution.py:391
  23.2 1.6 %collective-permute-start.5 = (f32[16,1,1024]{2,1,0:T(1,128)S(1)}, f32[16,1,1024]{2,1,0:T(1,128)S(1)}, u32[]{:S(2)}, u32[]{:S(2)}) collective-permute-start(f32[16,1,1024]{2,1,0:T(1,128)S(1)} %get-tuple-element.46), channel_id=1, source_target_pairs={{0,2},{2,0},{1,3},{3,1},{4,6},{6,4},{5,7},{7,5},{8,10},{10,8},{9,1... | collective-permute-start | bytes 196616 | tf_op jit(solution)/shard_map/ppermute | solution.py:404
  24.7 3.1 %collective-permute-done.5 = f32[16,1,1024]{2,1,0:T(1,128)S(1)} collective-permute-done((f32[16,1,1024]{2,1,0:T(1,128)S(1)}, f32[16,1,1024]{2,1,0:T(1,128)S(1)}, u32[]{:S(2)}, u32[]{:S(2)}) %collective-permute-start.5) | collective-permute-done | bytes 65568 | tf_op jit(solution)/shard_map/ppermute | solution.py:404
  27.8 0.7 %add.3 = f32[16,1,1024]{2,1,0:T(1,128)} add(f32[16,1,1024]{2,1,0:T(1,128)S(1)} %get-tuple-element.45, f32[16,1,1024]{2,1,0:T(1,128)S(1)} %collective-permute-done.5) | non-fusion elementwise | flops 16384 | bytes 196608 | tf_op jit(solution)/shard_map/add | solution.py:451
  (1 shorter events, 0.0 us)
Async XLA Ops:
  2.6 1.7 %collective-permute-start = (f32[128,512]{1,0:T(8,128)S(1)}, f32[128,512]{1,0:T(8,128)S(1)}, u32[]{:S(2)}, u32[]{:S(2)}) collective-permute-start(f32[128,512]{1,0:T(8,128)S(1)} %get-tuple-element.30), channel_id=1, source_target_pairs={{0,1},{1,0},{2,3},{3,2},{4,5},{5,4},{6,7},{7,6},{8,9},{9,8},{10,11... | collective-permute-start | bytes 786440 | tf_op jit(solution)/shard_map/ppermute | solution.py:404
  4.4 6.6 %collective-permute-start.1 = (f32[96,512]{1,0:T(8,128)S(1)}, f32[96,512]{1,0:T(8,128)S(1)}, u32[]{:S(2)}, u32[]{:S(2)}) collective-permute-start(f32[96,512]{1,0:T(8,128)S(1)} %make_messages.1), channel_id=1, source_target_pairs={{0,2},{2,0},{1,3},{3,1},{4,6},{6,4},{5,7},{7,5},{8,10},{10,8},{9,1... | collective-permute-start | bytes 589832 | tf_op jit(solution)/shard_map/ppermute | solution.py:404
  11.2 6.5 %collective-permute-start.4 = (f32[128,128]{1,0:T(8,128)S(1)}, f32[128,128]{1,0:T(8,128)S(1)}, u32[]{:S(2)}, u32[]{:S(2)}) collective-permute-start(f32[128,128]{1,0:T(8,128)S(1)} %outer_products.1.refs_0_), channel_id=1, source_target_pairs={{0,12},{1,13},{4,8},{5,9},{8,4},{9,5},{12,0},{13,1},{2,14},{3,15},... | collective-permute-start | bytes 196616 | tf_op jit(solution)/shard_map/ppermute | solution.py:414
  15.4 5.7 %collective-permute-start.3 = (f32[128,128]{1,0:T(8,128)S(1)}, f32[128,128]{1,0:T(8,128)S(1)}, u32[]{:S(2)}, u32[]{:S(2)}) collective-permute-start(f32[128,128]{1,0:T(8,128)S(1)} %outer_products.1.refs_0_), channel_id=1, source_target_pairs={{0,8},{1,5},{4,12},{5,1},{8,0},{9,13},{12,4},{13,9},{2,10},{3,7},{... | collective-permute-start | bytes 196616 | tf_op jit(solution)/shard_map/ppermute | solution.py:414
  15.4 5.7 %collective-permute-start.2 = (f32[128,128]{1,0:T(8,128)S(1)}, f32[128,128]{1,0:T(8,128)S(1)}, u32[]{:S(2)}, u32[]{:S(2)}) collective-permute-start(f32[128,128]{1,0:T(8,128)S(1)} %outer_products.1.refs_0_), channel_id=1, source_target_pairs={{0,4},{1,9},{4,0},{5,13},{8,12},{9,1},{12,8},{13,5},{2,6},{3,11},{... | collective-permute-start | bytes 196616 | tf_op jit(solution)/shard_map/ppermute | solution.py:414
  23.2 4.6 %collective-permute-start.5 = (f32[16,1,1024]{2,1,0:T(1,128)S(1)}, f32[16,1,1024]{2,1,0:T(1,128)S(1)}, u32[]{:S(2)}, u32[]{:S(2)}) collective-permute-start(f32[16,1,1024]{2,1,0:T(1,128)S(1)} %get-tuple-element.46), channel_id=1, source_target_pairs={{0,2},{2,0},{1,3},{3,1},{4,6},{6,4},{5,7},{7,5},{8,10},{10,8},{9,1... | collective-permute-start | bytes 196616 | tf_op jit(solution)/shard_map/ppermute | solution.py:404

commit v7 on v6

--- a/solution.py
+++ b/solution.py
@@ -352,16 +352,16 @@
     return list(zip(steps, sorted(steps, key=lambda step: (step.bit_count(), -step))))
 
 
-def fisher_kernel(wid_count, *refs):
-    seq_count = len(refs) - 3 - wid_count
+def fisher_kernel(*refs):
+    seq_count = len(refs) - 3
+    wid_count, owned = refs[-1].shape[:2]
     gathered = refs[:seq_count]
     high, low = refs[seq_count : seq_count + 2]
-    outs = refs[seq_count + 2 : seq_count + 2 + wid_count]
-    placed = refs[-1]
+    out = refs[-1]
     seq = lax.axis_index("seq")
     wid = lax.axis_index("wid")
     per_wid = seq_count // wid_count
-    sequences = placed.shape[2]
+    sequences = owned // per_wid
     steps = gathered[0].shape[0] // sequences
     rows = []
     for ref in gathered:
@@ -376,10 +376,8 @@
     for shift, (first, second) in enumerate([(0, 0)] + exchange_steps(seq_count)):
         group = seq ^ jnp.where(rep == 0, first, second)
         target = lax.rem(group // per_wid - wid + wid_count, wid_count)
-        placed[target, lax.rem(group, per_wid)] = result[shift * sequences : (shift + 1) * sequences]
-    for target, out in enumerate(outs):
-        for group in range(per_wid):
-            out[group * sequences : (group + 1) * sequences, 0, :] = placed[target, group]
+        rows = pl.ds(pl.multiple_of(lax.rem(group, per_wid) * sequences, sequences), sequences)
+        out[target, rows, 0, :] = result[shift * sequences : (shift + 1) * sequences]
 
 
 def fisher_product(gathered, high, low, wid_count):
@@ -387,13 +385,11 @@
     rows, columns = high.shape
     sequences = gathered[0].shape[0] * BLK // columns
     per_wid = seq_count // wid_count
-    shape = jax.ShapeDtypeStruct((per_wid * sequences, 1, rows), F32)
-    return pl.pallas_call(
-        functools.partial(fisher_kernel, wid_count),
-        out_shape=[shape] * wid_count,
+    return pl.pallas_call(
+        fisher_kernel,
+        out_shape=jax.ShapeDtypeStruct((wid_count, per_wid * sequences, 1, rows), F32),
         in_specs=[VMEM] * (seq_count + 2),
-        out_specs=[VMEM] * wid_count,
-        scratch_shapes=[pltpu.VMEM((wid_count, per_wid, sequences, rows), F32)],
+        out_specs=VMEM,
         compiler_params=PARAMS,
         name="fisher_product",
     )(*gathered, high, low)

time: 28.7 us -> 28.7 us (level)
  no operation moved by 1% of the time
where the time goes in v7:
time: 28.7 us; the launch traced here: 28.5 us
  starting transfers between devices  9.82 us (34%)
  Pallas kernels  9.21 us (32%)
  waiting for transfers between devices  8.74 us (30%)
  other arithmetic  0.7 us (2%)
    ppermute x3, waiting for transfers between devices, exchanged(): return lax.ppermute(value, ('seq', 'rep'), pairs)  5.02 us
    ppermute x3, starting transfers between devices, shifted(): lax.ppermute(value, axis, [(i, (i + shift) % count) for i in range(count)])  5 us
    ppermute x3, starting transfers between devices, exchanged(): return lax.ppermute(value, ('seq', 'rep'), pairs)  4.83 us
    pallas_call x2, Pallas kernels, split_fisher(): pl.pallas_call(split_late_kernel if halves else split_early_kernel, out_s...  3.72 us
    ppermute x3, waiting for transfers between devices, shifted(): lax.ppermute(value, axis, [(i, (i + shift) % count) for i in range(count)])  3.72 us
    pallas_call x1, Pallas kernels, project_other(): pl.pallas_call(project_other_kernel, out_shape=(jax.ShapeDtypeStruct((2 *...  2.64 us
    pallas_call x1, Pallas kernels, fisher_product(): pl.pallas_call(fisher_kernel, out_shape=jax.ShapeDtypeStruct((wid_count,...  2.1 us
    add x1, other arithmetic, shards(): result = result + shifted(parts[shift], 'wid', shift)  0.7 us
  transfers between devices with their start and end apart: 6, of which 4 were waited for; matrix products, arithmetic and copies ran while one was open for 0% of the time, Pallas kernels for 15%

profile of v7, /device:TPU:0, one launch (start us, length us, event | category | flops | bytes accessed | tf_op | source)
XLA Modules:
  0.0 28.5 jit_solution(4918739663247211699)
XLA Ops:
  0.0 2.6 %project_other.1 = (f32[128,512]{1,0:T(8,128)S(1)}, bf16[2,4,8,64,128]{4,3,2,1,0:T(8,128)(2,1)S(1)}, bf16[2,4,8,16,128]{4,3,2,1,0:T(8,128)(2,1)S(1)}, bf16[2,4,64,128]{3,2,1,0:T(8,128)(2,1)S(1)}) custom-call(s32[4]{0:T(128)} %act_index.1, s32[4]{0:T(128)} %grad_index.1, s32[16,16]{1,0:T(8,128)} %act_exponents.1, s32[16,16]{1,0:T(8,128)} %grad_exponents.1, ...), custom_call_target="tpu_custom_call" | custom-call | flops 67108864 | bytes 2359296 | tf_op jit(solution)/shard_map/project_other/pallas_call | solution.py:139
  2.6 0.5 %collective-permute-start = (f32[128,512]{1,0:T(8,128)S(1)}, f32[128,512]{1,0:T(8,128)S(1)}, u32[]{:S(2)}, u32[]{:S(2)}) collective-permute-start(f32[128,512]{1,0:T(8,128)S(1)} %get-tuple-element.28), channel_id=1, source_target_pairs={{0,1},{1,0},{2,3},{3,2},{4,5},{5,4},{6,7},{7,6},{8,9},{9,8},{10,11... | collective-permute-start | bytes 786440 | tf_op jit(solution)/shard_map/ppermute | solution.py:400
  3.2 0.4 %project_own.1.own = f32[128,512]{1,0:T(8,128)S(1)} custom-call(bf16[2,4,8,64,128]{4,3,2,1,0:T(8,128)(2,1)S(1)} %get-tuple-element.24.picked, bf16[2,4,8,16,128]{4,3,2,1,0:T(8,128)(2,1)S(1)} %get-tuple-element.25.scales, bf16[2,4,64,128]{3,2,1,0:T(8,128)(2,1)S(1)} %get-tuple-element.26.weights), custom_call_target="tpu_custom_call" | custom-call | flops 67108864 | bytes 1310720 | tf_op jit(solution)/shard_map/project_own/pallas_call | solution.py:178
  3.6 0.1 split_early.1
  3.7 0.6 %collective-permute-done.other = f32[128,512]{1,0:T(8,128)S(1)} collective-permute-done((f32[128,512]{1,0:T(8,128)S(1)}, f32[128,512]{1,0:T(8,128)S(1)}, u32[]{:S(2)}, u32[]{:S(2)}) %collective-permute-start) | collective-permute-done | bytes 262176 | tf_op jit(solution)/shard_map/ppermute | solution.py:400
  4.4 2.9 %collective-permute-start.1 = (f32[96,512]{1,0:T(8,128)S(1)}, f32[96,512]{1,0:T(8,128)S(1)}, u32[]{:S(2)}, u32[]{:S(2)}) collective-permute-start(f32[96,512]{1,0:T(8,128)S(1)} %make_messages.1), channel_id=1, source_target_pairs={{0,2},{2,0},{1,3},{3,1},{4,6},{6,4},{5,7},{7,5},{8,10},{10,8},{9,1... | collective-permute-start | bytes 589832 | tf_op jit(solution)/shard_map/ppermute | solution.py:400
  7.3 3.6 %split_late.1 = (bf16[1024,2048]{1,0:T(8,128)(2,1)S(1)}, bf16[1024,2048]{1,0:T(8,128)(2,1)S(1)}) custom-call(f32[1024,2048]{1,0:T(8,128)} %fisher.1, bf16[1024,2048]{1,0:T(8,128)(2,1)S(1)} %get-tuple-element.35.high_in, bf16[1024,2048]{1,0:T(8,128)(2,1)S(1)} %get-tuple-element.36.low_in), custom_call_target="tpu_custom_call" | custom-call | flops 4194304 | bytes 16777216 | tf_op jit(solution)/shard_map/split_late/pallas_call | solution.py:237
  10.9 0.0 collective-permute-done.1.rest_0_
  10.9 0.3 outer_products.1.refs_0_
  11.2 4.2 %collective-permute-start.4 = (f32[128,128]{1,0:T(8,128)S(1)}, f32[128,128]{1,0:T(8,128)S(1)}, u32[]{:S(2)}, u32[]{:S(2)}) collective-permute-start(f32[128,128]{1,0:T(8,128)S(1)} %outer_products.1.refs_0_), channel_id=1, source_target_pairs={{0,12},{1,13},{4,8},{5,9},{8,4},{9,5},{12,0},{13,1},{2,14},{3,15},... | collective-permute-start | bytes 196616 | tf_op jit(solution)/shard_map/ppermute | solution.py:410
  15.4 0.0 collective-permute-start.3
  15.4 0.6 %collective-permute-start.2 = (f32[128,128]{1,0:T(8,128)S(1)}, f32[128,128]{1,0:T(8,128)S(1)}, u32[]{:S(2)}, u32[]{:S(2)}) collective-permute-start(f32[128,128]{1,0:T(8,128)S(1)} %outer_products.1.refs_0_), channel_id=1, source_target_pairs={{0,4},{1,9},{4,0},{5,13},{8,12},{9,1},{12,8},{13,5},{2,6},{3,11},{... | collective-permute-start | bytes 196616 | tf_op jit(solution)/shard_map/ppermute | solution.py:410
  16.0 1.7 %collective-permute-done.4.refs_3_ = f32[128,128]{1,0:T(8,128)S(1)} collective-permute-done((f32[128,128]{1,0:T(8,128)S(1)}, f32[128,128]{1,0:T(8,128)S(1)}, u32[]{:S(2)}, u32[]{:S(2)}) %collective-permute-start.4) | collective-permute-done | bytes 65568 | tf_op jit(solution)/shard_map/ppermute | solution.py:410
  17.8 3.3 %collective-permute-done.3.refs_2_ = f32[128,128]{1,0:T(8,128)S(1)} collective-permute-done((f32[128,128]{1,0:T(8,128)S(1)}, f32[128,128]{1,0:T(8,128)S(1)}, u32[]{:S(2)}, u32[]{:S(2)}) %collective-permute-start.3) | collective-permute-done | bytes 65568 | tf_op jit(solution)/shard_map/ppermute | solution.py:410
  21.1 0.0 collective-permute-done.2.refs_1_
  21.1 2.1 %fisher_product.1 = f32[2,16,1,1024]{3,2,1,0:T(1,128)S(1)} custom-call(f32[128,128]{1,0:T(8,128)S(1)} %outer_products.1.refs_0_, f32[128,128]{1,0:T(8,128)S(1)} %collective-permute-done.2.refs_1_, f32[128,128]{1,0:T(8,128)S(1)} %collective-permute-done.3.refs_2_, f32[128,128]{1,0:T(8,128)S(1)} %collective-permute-done.4.refs_3_, ...), custom_call_target="tpu_custom_call" | custom-call | tf_op jit(solution)/shard_map/fisher_product/pallas_call | solution.py:388
  23.2 1.6 %collective-permute-start.5 = (f32[16,1,1024]{2,1,0:T(1,128)S(1)}, f32[16,1,1024]{2,1,0:T(1,128)S(1)}, u32[]{:S(2)}, u32[]{:S(2)}) collective-permute-start(f32[16,1,1024]{2,1,0:T(1,128)S(1)} %slice_bitcast_fusion), channel_id=1, source_target_pairs={{0,2},{2,0},{1,3},{3,1},{4,6},{6,4},{5,7},{7,5},{8,10},{10,8},{9,1... | collective-permute-start | bytes 196616 | tf_op jit(solution)/shard_map/ppermute | solution.py:400
  24.7 3.1 %collective-permute-done.5 = f32[16,1,1024]{2,1,0:T(1,128)S(1)} collective-permute-done((f32[16,1,1024]{2,1,0:T(1,128)S(1)}, f32[16,1,1024]{2,1,0:T(1,128)S(1)}, u32[]{:S(2)}, u32[]{:S(2)}) %collective-permute-start.5) | collective-permute-done | bytes 65568 | tf_op jit(solution)/shard_map/ppermute | solution.py:400
  27.8 0.7 %fusion = f32[16,1,1024]{2,1,0:T(1,128)} fusion(f32[16,1,1024]{2,1,0:T(1,128)S(1)} %collective-permute-done.5, f32[2,16,1,1024]{3,2,1,0:T(1,128)S(1)} %fisher_product.1), kind=kLoop, calls=%fused_computation.2 | loop fusion | flops 16384 | bytes 196608 | tf_op jit(solution)/shard_map/add | solution.py:447
  (2 shorter events, 0.0 us)
Async XLA Ops:
  2.6 1.7 %collective-permute-start = (f32[128,512]{1,0:T(8,128)S(1)}, f32[128,512]{1,0:T(8,128)S(1)}, u32[]{:S(2)}, u32[]{:S(2)}) collective-permute-start(f32[128,512]{1,0:T(8,128)S(1)} %get-tuple-element.28), channel_id=1, source_target_pairs={{0,1},{1,0},{2,3},{3,2},{4,5},{5,4},{6,7},{7,6},{8,9},{9,8},{10,11... | collective-permute-start | bytes 786440 | tf_op jit(solution)/shard_map/ppermute | solution.py:400
  4.4 6.6 %collective-permute-start.1 = (f32[96,512]{1,0:T(8,128)S(1)}, f32[96,512]{1,0:T(8,128)S(1)}, u32[]{:S(2)}, u32[]{:S(2)}) collective-permute-start(f32[96,512]{1,0:T(8,128)S(1)} %make_messages.1), channel_id=1, source_target_pairs={{0,2},{2,0},{1,3},{3,1},{4,6},{6,4},{5,7},{7,5},{8,10},{10,8},{9,1... | collective-permute-start | bytes 589832 | tf_op jit(solution)/shard_map/ppermute | solution.py:400
  11.2 6.5 %collective-permute-start.4 = (f32[128,128]{1,0:T(8,128)S(1)}, f32[128,128]{1,0:T(8,128)S(1)}, u32[]{:S(2)}, u32[]{:S(2)}) collective-permute-start(f32[128,128]{1,0:T(8,128)S(1)} %outer_products.1.refs_0_), channel_id=1, source_target_pairs={{0,12},{1,13},{4,8},{5,9},{8,4},{9,5},{12,0},{13,1},{2,14},{3,15},... | collective-permute-start | bytes 196616 | tf_op jit(solution)/shard_map/ppermute | solution.py:410
  15.4 5.7 %collective-permute-start.3 = (f32[128,128]{1,0:T(8,128)S(1)}, f32[128,128]{1,0:T(8,128)S(1)}, u32[]{:S(2)}, u32[]{:S(2)}) collective-permute-start(f32[128,128]{1,0:T(8,128)S(1)} %outer_products.1.refs_0_), channel_id=1, source_target_pairs={{0,8},{1,5},{4,12},{5,1},{8,0},{9,13},{12,4},{13,9},{2,10},{3,7},{... | collective-permute-start | bytes 196616 | tf_op jit(solution)/shard_map/ppermute | solution.py:410
  15.4 5.7 %collective-permute-start.2 = (f32[128,128]{1,0:T(8,128)S(1)}, f32[128,128]{1,0:T(8,128)S(1)}, u32[]{:S(2)}, u32[]{:S(2)}) collective-permute-start(f32[128,128]{1,0:T(8,128)S(1)} %outer_products.1.refs_0_), channel_id=1, source_target_pairs={{0,4},{1,9},{4,0},{5,13},{8,12},{9,1},{12,8},{13,5},{2,6},{3,11},{... | collective-permute-start | bytes 196616 | tf_op jit(solution)/shard_map/ppermute | solution.py:410
  23.2 4.6 %collective-permute-start.5 = (f32[16,1,1024]{2,1,0:T(1,128)S(1)}, f32[16,1,1024]{2,1,0:T(1,128)S(1)}, u32[]{:S(2)}, u32[]{:S(2)}) collective-permute-start(f32[16,1,1024]{2,1,0:T(1,128)S(1)} %slice_bitcast_fusion), channel_id=1, source_target_pairs={{0,2},{2,0},{1,3},{3,1},{4,6},{6,4},{5,7},{7,5},{8,10},{10,8},{9,1... | collective-permute-start | bytes 196616 | tf_op jit(solution)/shard_map/ppermute | solution.py:400

commit v8 on v7

--- a/solution.py
+++ b/solution.py
@@ -276,12 +276,12 @@
     )(own, other)
 
 
-def outer_kernel(width, own, other, *rest):
+def outer_kernel(width, own, other, sent, *rest):
     *messages, out, staged = rest
     wid = lax.axis_index("wid")
     share = width // (len(messages) + 1)
     rows = pl.ds(pl.multiple_of(width + wid * share, share), share)
-    acts = own[:width, :] + other[:width, :]
+    acts = sent[:width, :]
     grads = own[rows, :] + other[rows, :]
     for message in messages:
         acts = acts + message[:width, :]
@@ -306,7 +306,7 @@
         out[pl.ds(2 * pair + 1, half, stride=2 * pairs), :] = both[half:, :]
 
 
-def outer_products(own, other, messages):
+def outer_products(own, other, sent, messages):
     width = own.shape[0] // 2
     tokens = own.shape[1]
     share = width // (len(messages) + 1)
@@ -314,12 +314,12 @@
     return pl.pallas_call(
         functools.partial(outer_kernel, width),
         out_shape=jax.ShapeDtypeStruct((share // 2 * sequences, 2 * width), F32),
-        in_specs=[VMEM] * (2 + len(messages)),
+        in_specs=[VMEM] * (3 + len(messages)),
         out_specs=VMEM,
         scratch_shapes=[pltpu.VMEM((tokens // BLK, share, BLK), F32)],
         compiler_params=PARAMS,
         name="outer_products",
-    )(own, other, *messages)
+    )(own, other, sent, *messages)
 
 
 def tile_products(left_high, left_low, high, low):
@@ -439,7 +439,7 @@
     received = [shifted(m, "wid", shift) for shift, m in enumerate(messages, 1)]
     high, low = split_fisher(fisher, *halves)
     own, high, low = lax.optimization_barrier((own, high, low))
-    outer = outer_products(own, other, received)
+    outer = outer_products(own, other, messages[0], received)
     gathered = [outer] + [exchanged(outer, steps) for steps in exchange_steps(seq_count)]
     parts = fisher_product(gathered, high, low, wid_count)
     result = parts[0]

time: 28.7 us -> 28.7 us (level)
  no operation moved by 1% of the time
where the time goes in v8:
time: 28.7 us; the launch traced here: 28.5 us
  starting transfers between devices  9.82 us (34%)
  Pallas kernels  9.22 us (32%)
  waiting for transfers between devices  8.73 us (30%)
  other arithmetic  0.7 us (2%)
    ppermute x3, waiting for transfers between devices, exchanged(): return lax.ppermute(value, ('seq', 'rep'), pairs)  5.02 us
    ppermute x3, starting transfers between devices, shifted(): lax.ppermute(value, axis, [(i, (i + shift) % count) for i in range(count)])  5 us
    ppermute x3, starting transfers between devices, exchanged(): return lax.ppermute(value, ('seq', 'rep'), pairs)  4.82 us
    pallas_call x2, Pallas kernels, split_fisher(): pl.pallas_call(split_late_kernel if halves else split_early_kernel, out_s...  3.72 us
    ppermute x3, waiting for transfers between devices, shifted(): lax.ppermute(value, axis, [(i, (i + shift) % count) for i in range(count)])  3.71 us
    pallas_call x1, Pallas kernels, project_other(): pl.pallas_call(project_other_kernel, out_shape=(jax.ShapeDtypeStruct((2 *...  2.64 us
    pallas_call x1, Pallas kernels, fisher_product(): pl.pallas_call(fisher_kernel, out_shape=jax.ShapeDtypeStruct((wid_count,...  2.1 us
    add x1, other arithmetic, shards(): result = result + shifted(parts[shift], 'wid', shift)  0.7 us
  transfers between devices with their start and end apart: 6, of which 4 were waited for; matrix products, arithmetic and copies ran while one was open for 0% of the time, Pallas kernels for 15%

profile of v8, /device:TPU:0, one launch (start us, length us, event | category | flops | bytes accessed | tf_op | source)
XLA Modules:
  0.0 28.5 jit_solution(931811610899460870)
XLA Ops:
  0.0 2.6 %project_other.1 = (f32[128,512]{1,0:T(8,128)S(1)}, bf16[2,4,8,64,128]{4,3,2,1,0:T(8,128)(2,1)S(1)}, bf16[2,4,8,16,128]{4,3,2,1,0:T(8,128)(2,1)S(1)}, bf16[2,4,64,128]{3,2,1,0:T(8,128)(2,1)S(1)}) custom-call(s32[4]{0:T(128)} %act_index.1, s32[4]{0:T(128)} %grad_index.1, s32[16,16]{1,0:T(8,128)} %act_exponents.1, s32[16,16]{1,0:T(8,128)} %grad_exponents.1, ...), custom_call_target="tpu_custom_call" | custom-call | flops 67108864 | bytes 2359296 | tf_op jit(solution)/shard_map/project_other/pallas_call | solution.py:139
  2.6 0.5 %collective-permute-start = (f32[128,512]{1,0:T(8,128)S(1)}, f32[128,512]{1,0:T(8,128)S(1)}, u32[]{:S(2)}, u32[]{:S(2)}) collective-permute-start(f32[128,512]{1,0:T(8,128)S(1)} %get-tuple-element.28), channel_id=1, source_target_pairs={{0,1},{1,0},{2,3},{3,2},{4,5},{5,4},{6,7},{7,6},{8,9},{9,8},{10,11... | collective-permute-start | bytes 786440 | tf_op jit(solution)/shard_map/ppermute | solution.py:400
  3.2 0.4 %project_own.1.own = f32[128,512]{1,0:T(8,128)S(1)} custom-call(bf16[2,4,8,64,128]{4,3,2,1,0:T(8,128)(2,1)S(1)} %get-tuple-element.24.picked, bf16[2,4,8,16,128]{4,3,2,1,0:T(8,128)(2,1)S(1)} %get-tuple-element.25.scales, bf16[2,4,64,128]{3,2,1,0:T(8,128)(2,1)S(1)} %get-tuple-element.26.weights), custom_call_target="tpu_custom_call" | custom-call | flops 67108864 | bytes 1310720 | tf_op jit(solution)/shard_map/project_own/pallas_call | solution.py:178
  3.6 0.1 split_early.1
  3.7 0.6 %collective-permute-done.other = f32[128,512]{1,0:T(8,128)S(1)} collective-permute-done((f32[128,512]{1,0:T(8,128)S(1)}, f32[128,512]{1,0:T(8,128)S(1)}, u32[]{:S(2)}, u32[]{:S(2)}) %collective-permute-start) | collective-permute-done | bytes 262176 | tf_op jit(solution)/shard_map/ppermute | solution.py:400
  4.4 2.9 %collective-permute-start.1 = (f32[96,512]{1,0:T(8,128)S(1)}, f32[96,512]{1,0:T(8,128)S(1)}, u32[]{:S(2)}, u32[]{:S(2)}) collective-permute-start(f32[96,512]{1,0:T(8,128)S(1)} %make_messages.1.sent), channel_id=1, source_target_pairs={{0,2},{2,0},{1,3},{3,1},{4,6},{6,4},{5,7},{7,5},{8,10},{10,8},{9,1... | collective-permute-start | bytes 589832 | tf_op jit(solution)/shard_map/ppermute | solution.py:400
  7.3 3.6 %split_late.1 = (bf16[1024,2048]{1,0:T(8,128)(2,1)S(1)}, bf16[1024,2048]{1,0:T(8,128)(2,1)S(1)}) custom-call(f32[1024,2048]{1,0:T(8,128)} %fisher.1, bf16[1024,2048]{1,0:T(8,128)(2,1)S(1)} %get-tuple-element.35.high_in, bf16[1024,2048]{1,0:T(8,128)(2,1)S(1)} %get-tuple-element.36.low_in), custom_call_target="tpu_custom_call" | custom-call | flops 4194304 | bytes 16777216 | tf_op jit(solution)/shard_map/split_late/pallas_call | solution.py:237
  10.9 0.0 collective-permute-done.1.rest_0_
  10.9 0.3 %outer_products.1.refs_0_ = f32[128,128]{1,0:T(8,128)S(1)} custom-call(f32[128,512]{1,0:T(8,128)S(1)} %project_own.1.own, f32[128,512]{1,0:T(8,128)S(1)} %collective-permute-done.other, f32[96,512]{1,0:T(8,128)S(1)} %make_messages.1.sent, f32[96,512]{1,0:T(8,128)S(1)} %collective-permute-done.1.rest_0_), custom_call_target="tpu_custom_call" | custom-call | tf_op jit(solution)/shard_map/outer_products/pallas_call | solution.py:314
  11.2 4.2 %collective-permute-start.4 = (f32[128,128]{1,0:T(8,128)S(1)}, f32[128,128]{1,0:T(8,128)S(1)}, u32[]{:S(2)}, u32[]{:S(2)}) collective-permute-start(f32[128,128]{1,0:T(8,128)S(1)} %outer_products.1.refs_0_), channel_id=1, source_target_pairs={{0,12},{1,13},{4,8},{5,9},{8,4},{9,5},{12,0},{13,1},{2,14},{3,15},... | collective-permute-start | bytes 196616 | tf_op jit(solution)/shard_map/ppermute | solution.py:410
  15.4 0.0 collective-permute-start.3
  15.4 0.6 %collective-permute-start.2 = (f32[128,128]{1,0:T(8,128)S(1)}, f32[128,128]{1,0:T(8,128)S(1)}, u32[]{:S(2)}, u32[]{:S(2)}) collective-permute-start(f32[128,128]{1,0:T(8,128)S(1)} %outer_products.1.refs_0_), channel_id=1, source_target_pairs={{0,4},{1,9},{4,0},{5,13},{8,12},{9,1},{12,8},{13,5},{2,6},{3,11},{... | collective-permute-start | bytes 196616 | tf_op jit(solution)/shard_map/ppermute | solution.py:410
  16.0 1.7 %collective-permute-done.4.refs_3_ = f32[128,128]{1,0:T(8,128)S(1)} collective-permute-done((f32[128,128]{1,0:T(8,128)S(1)}, f32[128,128]{1,0:T(8,128)S(1)}, u32[]{:S(2)}, u32[]{:S(2)}) %collective-permute-start.4) | collective-permute-done | bytes 65568 | tf_op jit(solution)/shard_map/ppermute | solution.py:410
  17.8 3.3 %collective-permute-done.3.refs_2_ = f32[128,128]{1,0:T(8,128)S(1)} collective-permute-done((f32[128,128]{1,0:T(8,128)S(1)}, f32[128,128]{1,0:T(8,128)S(1)}, u32[]{:S(2)}, u32[]{:S(2)}) %collective-permute-start.3) | collective-permute-done | bytes 65568 | tf_op jit(solution)/shard_map/ppermute | solution.py:410
  21.1 0.0 collective-permute-done.2.refs_1_
  21.1 2.1 %fisher_product.1 = f32[2,16,1,1024]{3,2,1,0:T(1,128)S(1)} custom-call(f32[128,128]{1,0:T(8,128)S(1)} %outer_products.1.refs_0_, f32[128,128]{1,0:T(8,128)S(1)} %collective-permute-done.2.refs_1_, f32[128,128]{1,0:T(8,128)S(1)} %collective-permute-done.3.refs_2_, f32[128,128]{1,0:T(8,128)S(1)} %collective-permute-done.4.refs_3_, ...), custom_call_target="tpu_custom_call" | custom-call | tf_op jit(solution)/shard_map/fisher_product/pallas_call | solution.py:388
  23.2 1.6 %collective-permute-start.5 = (f32[16,1,1024]{2,1,0:T(1,128)S(1)}, f32[16,1,1024]{2,1,0:T(1,128)S(1)}, u32[]{:S(2)}, u32[]{:S(2)}) collective-permute-start(f32[16,1,1024]{2,1,0:T(1,128)S(1)} %slice_bitcast_fusion), channel_id=1, source_target_pairs={{0,2},{2,0},{1,3},{3,1},{4,6},{6,4},{5,7},{7,5},{8,10},{10,8},{9,1... | collective-permute-start | bytes 196616 | tf_op jit(solution)/shard_map/ppermute | solution.py:400
  24.7 3.1 %collective-permute-done.5 = f32[16,1,1024]{2,1,0:T(1,128)S(1)} collective-permute-done((f32[16,1,1024]{2,1,0:T(1,128)S(1)}, f32[16,1,1024]{2,1,0:T(1,128)S(1)}, u32[]{:S(2)}, u32[]{:S(2)}) %collective-permute-start.5) | collective-permute-done | bytes 65568 | tf_op jit(solution)/shard_map/ppermute | solution.py:400
  27.8 0.7 %fusion = f32[16,1,1024]{2,1,0:T(1,128)} fusion(f32[16,1,1024]{2,1,0:T(1,128)S(1)} %collective-permute-done.5, f32[2,16,1,1024]{3,2,1,0:T(1,128)S(1)} %fisher_product.1), kind=kLoop, calls=%fused_computation.2 | loop fusion | flops 16384 | bytes 196608 | tf_op jit(solution)/shard_map/add | solution.py:447
  (2 shorter events, 0.0 us)
Async XLA Ops:
  2.6 1.7 %collective-permute-start = (f32[128,512]{1,0:T(8,128)S(1)}, f32[128,512]{1,0:T(8,128)S(1)}, u32[]{:S(2)}, u32[]{:S(2)}) collective-permute-start(f32[128,512]{1,0:T(8,128)S(1)} %get-tuple-element.28), channel_id=1, source_target_pairs={{0,1},{1,0},{2,3},{3,2},{4,5},{5,4},{6,7},{7,6},{8,9},{9,8},{10,11... | collective-permute-start | bytes 786440 | tf_op jit(solution)/shard_map/ppermute | solution.py:400
  4.4 6.6 %collective-permute-start.1 = (f32[96,512]{1,0:T(8,128)S(1)}, f32[96,512]{1,0:T(8,128)S(1)}, u32[]{:S(2)}, u32[]{:S(2)}) collective-permute-start(f32[96,512]{1,0:T(8,128)S(1)} %make_messages.1.sent), channel_id=1, source_target_pairs={{0,2},{2,0},{1,3},{3,1},{4,6},{6,4},{5,7},{7,5},{8,10},{10,8},{9,1... | collective-permute-start | bytes 589832 | tf_op jit(solution)/shard_map/ppermute | solution.py:400
  11.2 6.5 %collective-permute-start.4 = (f32[128,128]{1,0:T(8,128)S(1)}, f32[128,128]{1,0:T(8,128)S(1)}, u32[]{:S(2)}, u32[]{:S(2)}) collective-permute-start(f32[128,128]{1,0:T(8,128)S(1)} %outer_products.1.refs_0_), channel_id=1, source_target_pairs={{0,12},{1,13},{4,8},{5,9},{8,4},{9,5},{12,0},{13,1},{2,14},{3,15},... | collective-permute-start | bytes 196616 | tf_op jit(solution)/shard_map/ppermute | solution.py:410
  15.4 5.7 %collective-permute-start.3 = (f32[128,128]{1,0:T(8,128)S(1)}, f32[128,128]{1,0:T(8,128)S(1)}, u32[]{:S(2)}, u32[]{:S(2)}) collective-permute-start(f32[128,128]{1,0:T(8,128)S(1)} %outer_products.1.refs_0_), channel_id=1, source_target_pairs={{0,8},{1,5},{4,12},{5,1},{8,0},{9,13},{12,4},{13,9},{2,10},{3,7},{... | collective-permute-start | bytes 196616 | tf_op jit(solution)/shard_map/ppermute | solution.py:410
  15.4 5.7 %collective-permute-start.2 = (f32[128,128]{1,0:T(8,128)S(1)}, f32[128,128]{1,0:T(8,128)S(1)}, u32[]{:S(2)}, u32[]{:S(2)}) collective-permute-start(f32[128,128]{1,0:T(8,128)S(1)} %outer_products.1.refs_0_), channel_id=1, source_target_pairs={{0,4},{1,9},{4,0},{5,13},{8,12},{9,1},{12,8},{13,5},{2,6},{3,11},{... | collective-permute-start | bytes 196616 | tf_op jit(solution)/shard_map/ppermute | solution.py:410
  23.2 4.6 %collective-permute-start.5 = (f32[16,1,1024]{2,1,0:T(1,128)S(1)}, f32[16,1,1024]{2,1,0:T(1,128)S(1)}, u32[]{:S(2)}, u32[]{:S(2)}) collective-permute-start(f32[16,1,1024]{2,1,0:T(1,128)S(1)} %slice_bitcast_fusion), channel_id=1, source_target_pairs={{0,2},{2,0},{1,3},{3,1},{4,6},{6,4},{5,7},{7,5},{8,10},{10,8},{9,1... | collective-permute-start | bytes 196616 | tf_op jit(solution)/shard_map/ppermute | solution.py:400

commit v9 on v7

--- a/solution.py
+++ b/solution.py
@@ -325,6 +325,7 @@
 def tile_products(left_high, left_low, high, low):
     rows, columns = high.shape
     streamed = rows // 4 // MXU * MXU
+    middle = streamed + MXU if streamed else rows // 2
     count = left_high.shape[0]
     both = jnp.concatenate([left_high, left_low], axis=0)
     dot = functools.partial(lax.dot_general, dimension_numbers=NT, preferred_element_type=F32)
@@ -332,17 +333,21 @@
     for start in range(0, columns, MXU):
         piece = slice(start, start + MXU)
         terms = []
+        terms.append(dot(both[:, piece], high[streamed:middle, piece]))
         if streamed:
             terms.append(dot(high[:streamed, piece], both[:, piece]))
-        terms.append(dot(both[:, piece], high[streamed:, piece]))
+        terms.append(dot(both[:, piece], high[middle:, piece]))
         if streamed:
             terms.append(dot(low[:streamed, piece], left_high[:, piece]))
-        terms.append(dot(left_high[:, piece], low[streamed:, piece]))
+        terms.append(dot(left_high[:, piece], low[streamed:middle, piece]))
+        terms.append(dot(left_high[:, piece], low[middle:, piece]))
         sums = terms if sums is None else [a + b for a, b in zip(sums, terms)]
-    held_high, held_low = sums[1::2] if streamed else sums
+    tall_high, tall_low = (sums.pop(1), sums.pop(2)) if streamed else (None, None)
+    held_high = jnp.concatenate(sums[:2], axis=1)
+    held_low = jnp.concatenate(sums[2:], axis=1)
     result = held_high[:count] + (held_high[count:] + held_low)
     if streamed:
-        tall = sums[0][:, :count] + (sums[0][:, count:] + sums[2])
+        tall = tall_high[:, :count] + (tall_high[:, count:] + tall_low)
         result = jnp.concatenate([tall.T, result], axis=1)
     return result
 

time: 28.7 us -> 28.7 us (level)
  no operation moved by 1% of the time
where the time goes in v9:
time: 28.7 us; the launch traced here: 28.5 us
  starting transfers between devices  9.82 us (34%)
  Pallas kernels  9.22 us (32%)
  waiting for transfers between devices  8.74 us (30%)
  other arithmetic  0.7 us (2%)
    ppermute x3, waiting for transfers between devices, exchanged(): return lax.ppermute(value, ('seq', 'rep'), pairs)  5.02 us
    ppermute x3, starting transfers between devices, shifted(): lax.ppermute(value, axis, [(i, (i + shift) % count) for i in range(count)])  5 us
    ppermute x3, starting transfers between devices, exchanged(): return lax.ppermute(value, ('seq', 'rep'), pairs)  4.83 us
    pallas_call x2, Pallas kernels, split_fisher(): pl.pallas_call(split_late_kernel if halves else split_early_kernel, out_s...  3.72 us
    ppermute x3, waiting for transfers between devices, shifted(): lax.ppermute(value, axis, [(i, (i + shift) % count) for i in range(count)])  3.72 us
    pallas_call x1, Pallas kernels, project_other(): pl.pallas_call(project_other_kernel, out_shape=(jax.ShapeDtypeStruct((2 *...  2.64 us
    pallas_call x1, Pallas kernels, fisher_product(): pl.pallas_call(fisher_kernel, out_shape=jax.ShapeDtypeStruct((wid_count,...  2.11 us
    add x1, other arithmetic, shards(): result = result + shifted(parts[shift], 'wid', shift)  0.7 us
  transfers between devices with their start and end apart: 6, of which 4 were waited for; matrix products, arithmetic and copies ran while one was open for 0% of the time, Pallas kernels for 15%

profile of v9, /device:TPU:0, one launch (start us, length us, event | category | flops | bytes accessed | tf_op | source)
XLA Modules:
  0.0 28.5 jit_solution(15706253741587624396)
XLA Ops:
  0.0 2.6 %project_other.1 = (f32[128,512]{1,0:T(8,128)S(1)}, bf16[2,4,8,64,128]{4,3,2,1,0:T(8,128)(2,1)S(1)}, bf16[2,4,8,16,128]{4,3,2,1,0:T(8,128)(2,1)S(1)}, bf16[2,4,64,128]{3,2,1,0:T(8,128)(2,1)S(1)}) custom-call(s32[4]{0:T(128)} %act_index.1, s32[4]{0:T(128)} %grad_index.1, s32[16,16]{1,0:T(8,128)} %act_exponents.1, s32[16,16]{1,0:T(8,128)} %grad_exponents.1, ...), custom_call_target="tpu_custom_call" | custom-call | flops 67108864 | bytes 2359296 | tf_op jit(solution)/shard_map/project_other/pallas_call | solution.py:139
  2.6 0.5 %collective-permute-start = (f32[128,512]{1,0:T(8,128)S(1)}, f32[128,512]{1,0:T(8,128)S(1)}, u32[]{:S(2)}, u32[]{:S(2)}) collective-permute-start(f32[128,512]{1,0:T(8,128)S(1)} %get-tuple-element.28), channel_id=1, source_target_pairs={{0,1},{1,0},{2,3},{3,2},{4,5},{5,4},{6,7},{7,6},{8,9},{9,8},{10,11... | collective-permute-start | bytes 786440 | tf_op jit(solution)/shard_map/ppermute | solution.py:405
  3.2 0.4 %project_own.1.own = f32[128,512]{1,0:T(8,128)S(1)} custom-call(bf16[2,4,8,64,128]{4,3,2,1,0:T(8,128)(2,1)S(1)} %get-tuple-element.24.picked, bf16[2,4,8,16,128]{4,3,2,1,0:T(8,128)(2,1)S(1)} %get-tuple-element.25.scales, bf16[2,4,64,128]{3,2,1,0:T(8,128)(2,1)S(1)} %get-tuple-element.26.weights), custom_call_target="tpu_custom_call" | custom-call | flops 67108864 | bytes 1310720 | tf_op jit(solution)/shard_map/project_own/pallas_call | solution.py:178
  3.6 0.1 split_early.1
  3.7 0.6 %collective-permute-done.other = f32[128,512]{1,0:T(8,128)S(1)} collective-permute-done((f32[128,512]{1,0:T(8,128)S(1)}, f32[128,512]{1,0:T(8,128)S(1)}, u32[]{:S(2)}, u32[]{:S(2)}) %collective-permute-start) | collective-permute-done | bytes 262176 | tf_op jit(solution)/shard_map/ppermute | solution.py:405
  4.4 2.9 %collective-permute-start.1 = (f32[96,512]{1,0:T(8,128)S(1)}, f32[96,512]{1,0:T(8,128)S(1)}, u32[]{:S(2)}, u32[]{:S(2)}) collective-permute-start(f32[96,512]{1,0:T(8,128)S(1)} %make_messages.1), channel_id=1, source_target_pairs={{0,2},{2,0},{1,3},{3,1},{4,6},{6,4},{5,7},{7,5},{8,10},{10,8},{9,1... | collective-permute-start | bytes 589832 | tf_op jit(solution)/shard_map/ppermute | solution.py:405
  7.3 3.6 %split_late.1 = (bf16[1024,2048]{1,0:T(8,128)(2,1)S(1)}, bf16[1024,2048]{1,0:T(8,128)(2,1)S(1)}) custom-call(f32[1024,2048]{1,0:T(8,128)} %fisher.1, bf16[1024,2048]{1,0:T(8,128)(2,1)S(1)} %get-tuple-element.35.high_in, bf16[1024,2048]{1,0:T(8,128)(2,1)S(1)} %get-tuple-element.36.low_in), custom_call_target="tpu_custom_call" | custom-call | flops 4194304 | bytes 16777216 | tf_op jit(solution)/shard_map/split_late/pallas_call | solution.py:237
  10.9 0.0 collective-permute-done.1.rest_0_
  10.9 0.3 outer_products.1.refs_0_
  11.2 4.2 %collective-permute-start.4 = (f32[128,128]{1,0:T(8,128)S(1)}, f32[128,128]{1,0:T(8,128)S(1)}, u32[]{:S(2)}, u32[]{:S(2)}) collective-permute-start(f32[128,128]{1,0:T(8,128)S(1)} %outer_products.1.refs_0_), channel_id=1, source_target_pairs={{0,12},{1,13},{4,8},{5,9},{8,4},{9,5},{12,0},{13,1},{2,14},{3,15},... | collective-permute-start | bytes 196616 | tf_op jit(solution)/shard_map/ppermute | solution.py:415
  15.4 0.0 collective-permute-start.3
  15.4 0.6 %collective-permute-start.2 = (f32[128,128]{1,0:T(8,128)S(1)}, f32[128,128]{1,0:T(8,128)S(1)}, u32[]{:S(2)}, u32[]{:S(2)}) collective-permute-start(f32[128,128]{1,0:T(8,128)S(1)} %outer_products.1.refs_0_), channel_id=1, source_target_pairs={{0,4},{1,9},{4,0},{5,13},{8,12},{9,1},{12,8},{13,5},{2,6},{3,11},{... | collective-permute-start | bytes 196616 | tf_op jit(solution)/shard_map/ppermute | solution.py:415
  16.0 1.7 %collective-permute-done.4.refs_3_ = f32[128,128]{1,0:T(8,128)S(1)} collective-permute-done((f32[128,128]{1,0:T(8,128)S(1)}, f32[128,128]{1,0:T(8,128)S(1)}, u32[]{:S(2)}, u32[]{:S(2)}) %collective-permute-start.4) | collective-permute-done | bytes 65568 | tf_op jit(solution)/shard_map/ppermute | solution.py:415
  17.8 3.3 %collective-permute-done.3.refs_2_ = f32[128,128]{1,0:T(8,128)S(1)} collective-permute-done((f32[128,128]{1,0:T(8,128)S(1)}, f32[128,128]{1,0:T(8,128)S(1)}, u32[]{:S(2)}, u32[]{:S(2)}) %collective-permute-start.3) | collective-permute-done | bytes 65568 | tf_op jit(solution)/shard_map/ppermute | solution.py:415
  21.1 0.0 collective-permute-done.2.refs_1_
  21.1 2.1 %fisher_product.1 = f32[2,16,1,1024]{3,2,1,0:T(1,128)S(1)} custom-call(f32[128,128]{1,0:T(8,128)S(1)} %outer_products.1.refs_0_, f32[128,128]{1,0:T(8,128)S(1)} %collective-permute-done.2.refs_1_, f32[128,128]{1,0:T(8,128)S(1)} %collective-permute-done.3.refs_2_, f32[128,128]{1,0:T(8,128)S(1)} %collective-permute-done.4.refs_3_, ...), custom_call_target="tpu_custom_call" | custom-call | tf_op jit(solution)/shard_map/fisher_product/pallas_call | solution.py:393
  23.2 1.6 %collective-permute-start.5 = (f32[16,1,1024]{2,1,0:T(1,128)S(1)}, f32[16,1,1024]{2,1,0:T(1,128)S(1)}, u32[]{:S(2)}, u32[]{:S(2)}) collective-permute-start(f32[16,1,1024]{2,1,0:T(1,128)S(1)} %slice_bitcast_fusion), channel_id=1, source_target_pairs={{0,2},{2,0},{1,3},{3,1},{4,6},{6,4},{5,7},{7,5},{8,10},{10,8},{9,1... | collective-permute-start | bytes 196616 | tf_op jit(solution)/shard_map/ppermute | solution.py:405
  24.8 3.1 %collective-permute-done.5 = f32[16,1,1024]{2,1,0:T(1,128)S(1)} collective-permute-done((f32[16,1,1024]{2,1,0:T(1,128)S(1)}, f32[16,1,1024]{2,1,0:T(1,128)S(1)}, u32[]{:S(2)}, u32[]{:S(2)}) %collective-permute-start.5) | collective-permute-done | bytes 65568 | tf_op jit(solution)/shard_map/ppermute | solution.py:405
  27.8 0.7 %fusion = f32[16,1,1024]{2,1,0:T(1,128)} fusion(f32[16,1,1024]{2,1,0:T(1,128)S(1)} %collective-permute-done.5, f32[2,16,1,1024]{3,2,1,0:T(1,128)S(1)} %fisher_product.1), kind=kLoop, calls=%fused_computation.2 | loop fusion | flops 16384 | bytes 196608 | tf_op jit(solution)/shard_map/add | solution.py:452
  (2 shorter events, 0.0 us)
Async XLA Ops:
  2.6 1.7 %collective-permute-start = (f32[128,512]{1,0:T(8,128)S(1)}, f32[128,512]{1,0:T(8,128)S(1)}, u32[]{:S(2)}, u32[]{:S(2)}) collective-permute-start(f32[128,512]{1,0:T(8,128)S(1)} %get-tuple-element.28), channel_id=1, source_target_pairs={{0,1},{1,0},{2,3},{3,2},{4,5},{5,4},{6,7},{7,6},{8,9},{9,8},{10,11... | collective-permute-start | bytes 786440 | tf_op jit(solution)/shard_map/ppermute | solution.py:405
  4.4 6.6 %collective-permute-start.1 = (f32[96,512]{1,0:T(8,128)S(1)}, f32[96,512]{1,0:T(8,128)S(1)}, u32[]{:S(2)}, u32[]{:S(2)}) collective-permute-start(f32[96,512]{1,0:T(8,128)S(1)} %make_messages.1), channel_id=1, source_target_pairs={{0,2},{2,0},{1,3},{3,1},{4,6},{6,4},{5,7},{7,5},{8,10},{10,8},{9,1... | collective-permute-start | bytes 589832 | tf_op jit(solution)/shard_map/ppermute | solution.py:405
  11.2 6.5 %collective-permute-start.4 = (f32[128,128]{1,0:T(8,128)S(1)}, f32[128,128]{1,0:T(8,128)S(1)}, u32[]{:S(2)}, u32[]{:S(2)}) collective-permute-start(f32[128,128]{1,0:T(8,128)S(1)} %outer_products.1.refs_0_), channel_id=1, source_target_pairs={{0,12},{1,13},{4,8},{5,9},{8,4},{9,5},{12,0},{13,1},{2,14},{3,15},... | collective-permute-start | bytes 196616 | tf_op jit(solution)/shard_map/ppermute | solution.py:415
  15.4 5.7 %collective-permute-start.3 = (f32[128,128]{1,0:T(8,128)S(1)}, f32[128,128]{1,0:T(8,128)S(1)}, u32[]{:S(2)}, u32[]{:S(2)}) collective-permute-start(f32[128,128]{1,0:T(8,128)S(1)} %outer_products.1.refs_0_), channel_id=1, source_target_pairs={{0,8},{1,5},{4,12},{5,1},{8,0},{9,13},{12,4},{13,9},{2,10},{3,7},{... | collective-permute-start | bytes 196616 | tf_op jit(solution)/shard_map/ppermute | solution.py:415
  15.4 5.7 %collective-permute-start.2 = (f32[128,128]{1,0:T(8,128)S(1)}, f32[128,128]{1,0:T(8,128)S(1)}, u32[]{:S(2)}, u32[]{:S(2)}) collective-permute-start(f32[128,128]{1,0:T(8,128)S(1)} %outer_products.1.refs_0_), channel_id=1, source_target_pairs={{0,4},{1,9},{4,0},{5,13},{8,12},{9,1},{12,8},{13,5},{2,6},{3,11},{... | collective-permute-start | bytes 196616 | tf_op jit(solution)/shard_map/ppermute | solution.py:415
  23.2 4.6 %collective-permute-start.5 = (f32[16,1,1024]{2,1,0:T(1,128)S(1)}, f32[16,1,1024]{2,1,0:T(1,128)S(1)}, u32[]{:S(2)}, u32[]{:S(2)}) collective-permute-start(f32[16,1,1024]{2,1,0:T(1,128)S(1)} %slice_bitcast_fusion), channel_id=1, source_target_pairs={{0,2},{2,0},{1,3},{3,1},{4,6},{6,4},{5,7},{7,5},{8,10},{10,8},{9,1... | collective-permute-start | bytes 196616 | tf_op jit(solution)/shard_map/ppermute | solution.py:405
